TPU v7x, 256 devices: a whole 4x4x8 slice. The times are simulated.
256 devices in a mesh: gx: 8 (over y, core), gy: 8 (over z), gz: 4 (over x).
Axes of the slice: x: 4, y: 4, z: 8, core: 2. Of those that a mesh axis runs over, the one named last changes fastest.
Arguments:
- offsets: float32 [3, 16, 32, 16, 128], P(None, 'gx', 'gy', 'gz'), may hold values from -1 to 1
- velocity: float32 [3, 16, 32, 16, 128], P(None, 'gx', 'gy', 'gz'), may hold values from -3 to 3
- mass: float32 [16, 32, 16, 128], P('gx', 'gy', 'gz'), may hold values from 0.03 to 0.09
- counts: int32 [16, 32, 16], P('gx', 'gy', 'gz'), may hold values from 1 to 128
- owner: int32 [8192, 1], P(('gx', 'gy', 'gz')), may hold values from 0 to 63; in each aligned block of 32 rows (0 to 31, 32 to 63, ...) at most 2 rows name the same one
Outputs:
- arrived: float32 [32768, 7, 128], P(('gx', 'gy', 'gz'))
- density: float32 [16, 32, 16, 128], P('gx', 'gy', 'gz')
Inputs may be any that keep to these rules, and one draw needn't show every extreme that they name: An owner is the layer index lx * 8 + ly of a device in the same gz layer. No device hands more than 2 bins to one owner, and some device hands exactly 2 to one.
All inputs are finite; a program needn't handle non-finite values.
Results may differ from a plain program's by a relative error of at most 0.0001.
Values sent between devices are 32-bit elements; how exact they have to be, the bound alone decides.
No kernel may reach another device: no remote copies, remote signals or barrier semaphores. Data moves between devices by JAX's collectives and lax.ppermute only.
A program may use at most 64 MiB of HBM per device.

v0:
```python
import math

import jax
import jax.numpy as jnp
import numpy as np
from jax import lax
from jax.sharding import PartitionSpec as P

SUBSTEPS = 2


ALPHA = 21.0 / (16.0 * math.pi)
STIFF = 0.002
RHO_REST = 0.15
FLOOR = 0.05
VISCOSITY = 0.1
GRAVITY = 1.0
TIMESTEP = 0.2


def extended(value, sides, width):
    for axis, dim in sides:
        devices, length = (lax.axis_size(axis), value.shape[dim])
        up = [(i, (i + 1) % devices) for i in range(devices - 1)]
        down = [(j, i) for i, j in up]
        last = lax.slice_in_dim(value, length - width, length, axis=dim)
        initial = lax.slice_in_dim(value, 0, width, axis=dim)
        before = lax.ppermute(last, axis, up)
        after = lax.ppermute(initial, axis, down)
        value = jnp.concatenate([before, value, after], axis=dim)
    return value


def displacements():
    return [(a, b, c) for a in (-1, 0, 1) for b in (-1, 0, 1) for c in (-1, 0, 1)]


def shift_table():
    return jnp.asarray(2.0 * np.array(displacements(), np.float32))


def neighbourhood(padded, grid):
    extent_x, extent_y, extent_z = grid
    fields = padded.shape[0]
    pieces = [
        padded[
            :, 1 + a : 1 + a + extent_x, 1 + b : 1 + b + extent_y, 1 + c : 1 + c + extent_z
        ].reshape(fields, extent_x * extent_y * extent_z, -1)
        for a, b, c in displacements()
    ]
    return jnp.stack(pieces, 0)


def geometry(own_pos, near_pos, shift):
    relative = own_pos[:, :, :, None] - (near_pos + shift[:, None, None])[:, :, None, :]
    dist_sq = jnp.sum(relative * relative, axis=0)
    distance = jnp.sqrt(dist_sq)
    falloff = jnp.maximum(1.0 - 0.5 * distance, 0.0)
    return (relative, dist_sq, distance, falloff)


def density_pair(own_pos, near_pos, near_mass, shift):
    relative, dist_sq, distance, falloff = geometry(own_pos, near_pos, shift)
    fall_sq = falloff * falloff
    kernel = ALPHA * fall_sq * fall_sq * (2.0 * distance + 1.0)
    return jnp.sum(near_mass[:, None, :] * kernel, axis=2)


def pressure_term(density):
    ratio = density / RHO_REST
    ratio_sq = ratio * ratio
    seventh = ratio_sq * ratio_sq * ratio_sq * ratio
    return STIFF * (seventh - 1.0) / (density * density)


def accel_pair(own_pos, own_vel, own_rho, near_pos, near_vel, near_mass, near_rho, shift):
    relative, dist_sq, distance, falloff = geometry(own_pos, near_pos, shift)
    near_rho = jnp.maximum(near_rho, FLOOR)
    approach = jnp.minimum(
        jnp.sum((own_vel[:, :, :, None] - near_vel[:, :, None, :]) * relative, axis=0), 0.0
    )
    mean_rho = 0.5 * (own_rho[:, :, None] + near_rho[:, None, :])
    viscous = -VISCOSITY * approach / ((dist_sq + 0.01) * mean_rho)
    slope = -5.0 * ALPHA * falloff * falloff * falloff
    weight = (
        near_mass[:, None, :]
        * (pressure_term(own_rho)[:, :, None] + pressure_term(near_rho)[:, None, :] + viscous)
        * slope
    )
    return -jnp.sum(weight[None] * relative, axis=3)


def blocked(kernel_fn, arrays, bins, block, out_axis):

    def one_block(number):
        pieces = [array for array in arrays]
        return kernel_fn(*pieces)

    result = lax.map(one_block, jnp.arange(bins // block, dtype=jnp.int32))
    result = jnp.moveaxis(result, 0, out_axis)
    shape = result.shape
    return result.reshape(
        shape[:out_axis] + (shape[out_axis] * shape[out_axis + 1],) + shape[out_axis + 2 :]
    )


def sum_density(own_pos, near_pos, near_mass, bins, block):

    def turn(total, item):
        each_pos, each_mass, shift = item
        term = blocked(
            lambda o, n, m: density_pair(o, n, m, shift),
            (own_pos, each_pos, each_mass),
            bins,
            block,
            0,
        )
        return (total + term, None)

    start = jnp.zeros(own_pos.shape[1:], jnp.float32)
    return lax.scan(turn, start, (near_pos, near_mass, shift_table()))[0]


def sum_accel(own_pos, own_vel, own_rho, near_pos, near_vel, near_mass, near_rho, bins, block):

    def turn(total, item):
        each_pos, each_vel, each_mass, each_rho, shift = item
        term = blocked(
            lambda a, b, c, d, e, f, g: accel_pair(a, b, c, d, e, f, g, shift),
            (own_pos, own_vel, own_rho, each_pos, each_vel, each_mass, each_rho),
            bins,
            block,
            1,
        )
        return (total + term, None)

    start = jnp.zeros(own_pos.shape, jnp.float32)
    return lax.scan(turn, start, (near_pos, near_vel, near_mass, near_rho, shift_table()))[0]


def local(offsets, velocity, mass, counts, owner):
    grid = counts.shape
    slots = mass.shape[-1]
    bins = grid[0] * grid[1] * grid[2]
    block = min(32, bins)
    slot_ids = jnp.arange(slots, dtype=jnp.int32)
    alive = (slot_ids[None, None, None, :] < counts[..., None]).astype(jnp.float32)
    states = jnp.concatenate(
        [offsets * alive[None], velocity * alive[None], (mass * alive)[None]], 0
    )
    alive_flat = alive.reshape(bins, slots)
    density = jnp.zeros((bins, slots), jnp.float32)
    downward = jnp.stack(
        [jnp.zeros((), jnp.float32), jnp.zeros((), jnp.float32), jnp.full((), GRAVITY, jnp.float32)]
    )
    for substep in range(SUBSTEPS):
        flattened = states.reshape(7, bins, slots)
        padded = extended(
            jnp.concatenate([states[0:3], states[6:7]], 0), (("gx", 1), ("gy", 2), ("gz", 3)), 1
        )
        nearby = neighbourhood(padded, grid)
        near_mass = nearby[:, 3]
        summed = sum_density(flattened[0:3], nearby[:, 0:3], near_mass, bins, block)
        density = jnp.maximum(summed, FLOOR)
        with_rho = jnp.concatenate([states, density.reshape((1,) + grid + (slots,))], 0)
        padded_all = extended(with_rho, (("gx", 1), ("gy", 2), ("gz", 3)), 1)
        near_all = neighbourhood(padded_all, grid)
        near_pos = near_all[:, 0:3]
        near_vel = near_all[:, 3:6]
        near_mass = near_all[:, 6]
        near_rho = near_all[:, 7]
        pulled = sum_accel(
            flattened[0:3],
            flattened[3:6],
            density,
            near_pos,
            near_vel,
            near_mass,
            near_rho,
            bins,
            block,
        )
        accel = (pulled - downward[:, None, None]) * alive_flat[None]
        velocity_now = flattened[3:6] + TIMESTEP * accel
        position_now = flattened[0:3] + TIMESTEP * velocity_now
        states = jnp.concatenate([position_now, velocity_now, flattened[6:7]], 0).reshape(
            (7,) + grid + (slots,)
        )
    size_gx = lax.axis_size("gx")
    size_gy = lax.axis_size("gy")
    layers = size_gx * size_gy
    capacity = max(2, 2 * bins // layers)
    target = owner[:, 0]
    one_hot = (target[:, None] == jnp.arange(layers, dtype=jnp.int32)[None, :]).astype(jnp.int32)
    rank = jnp.sum((jnp.cumsum(one_hot, axis=0) - one_hot) * one_hot, axis=1)
    where_to = target * capacity + rank
    selector = (
        where_to[None, :] == jnp.arange(layers * capacity, dtype=jnp.int32)[:, None]
    ).astype(jnp.float32)
    outgoing = jnp.einsum(
        "sb,fbp->sfp", selector, states.reshape(7, bins, slots), precision=lax.Precision.HIGHEST
    )
    arrived = lax.all_to_all(outgoing, ("gx", "gy"), split_axis=0, concat_axis=0, tiled=True)
    return (arrived, density.reshape(grid + (slots,)))


def solution(mesh):
    placed = (
        P(None, "gx", "gy", "gz", None),
        P(None, "gx", "gy", "gz", None),
        P("gx", "gy", "gz", None),
        P("gx", "gy", "gz"),
        P(("gx", "gy", "gz"), None),
    )
    return jax.shard_map(
        local,
        mesh=mesh,
        in_specs=placed,
        out_specs=(P(("gx", "gy", "gz"), None, None), P("gx", "gy", "gz", None)),
        check_vma=False,
    )
```

profile of v0, /device:TPU:10, one launch (start us, length us, event | category | flops | bytes accessed | tf_op | source)
XLA Modules:
  0.0 989.4 jit_solution(18209104207407051641)
XLA Ops:
  11.6 4.5 collective-permute-start.2
  27.8 113.7 %while.70 = (s32[]{:T(128)}, f32[32,128]{1,0:T(8,128)S(1)}, f32[27,32,128]{2,1,0:T(8,128)S(1)}, f32[3,32,128]{2,1,0:T(8,128)S(1)}, f32[27,3,32,128]{3,2,1,0:T(8,...) while((s32[]{:T(128)}, f32[32,128]{1,0:T(8,128)S(1)}, ...), condition=%wide.region_5.6_spmd.clone.clone, body=%wide.region_2.5_spmd.sunk.clone.clone.sunk | while | flops 9977859 | bytes 4505751 | solution.py:121
  150.5 4.9 collective-permute-start.8
  168.2 310.1 %while.71 = (s32[]{:T(128)}, f32[3,32,128]{2,1,0:T(8,128)S(1)}, f32[27,32,128]{2,1,0:T(8,128)S(1)}, f32[32,128]{1,0:T(8,128)S(1)}, f32[32,128,1]{1,0,2:T(8,128)S...) while((s32[]{:T(128)}, f32[3,32,128]{2,1,0:T(8,128)S(1)}, ...), condition=%wide.region_10.11_spmd.clone.clone, body=%wide.region_6.10_spmd.sunk.clone.clone.sunk | while | flops 22130688 | bytes 13484231 | solution.py:138
  169.0 4.2 fusion.214
  180.5 4.2 fusion.214
  192.0 4.2 fusion.214
  203.5 4.2 fusion.214
  215.0 4.2 fusion.214
  226.5 4.2 fusion.214
  237.9 4.2 fusion.214
  249.4 4.2 fusion.214
  260.9 4.2 fusion.214
  272.4 4.2 fusion.214
  283.9 4.2 fusion.214
  295.4 4.2 fusion.214
  306.9 4.2 fusion.214
  318.3 4.2 fusion.214
  329.8 4.2 fusion.214
  341.3 4.2 fusion.214
  352.8 4.2 fusion.214
  364.3 4.2 fusion.214
  375.8 4.2 fusion.214
  387.2 4.2 fusion.214
  398.7 4.2 fusion.214
  410.2 4.2 fusion.214
  487.0 4.9 collective-permute-start.14
  502.4 113.7 %while.72 = (s32[]{:T(128)}, f32[32,128]{1,0:T(8,128)S(1)}, f32[27,32,128]{2,1,0:T(8,128)S(1)}, f32[3,32,128]{2,1,0:T(8,128)S(1)}, f32[27,3,32,128]{3,2,1,0:T(8,...) while((s32[]{:T(128)}, f32[32,128]{1,0:T(8,128)S(1)}, ...), condition=%wide.region_14.15_spmd.clone.clone, body=%wide.region_11.14_spmd.sunk.clone.clone.sunk | while | flops 9977859 | bytes 4505751 | solution.py:121
  625.1 4.9 collective-permute-start.20
  642.9 310.1 %while.73 = (s32[]{:T(128)}, f32[3,32,128]{2,1,0:T(8,128)S(1)}, f32[27,32,128]{2,1,0:T(8,128)S(1)}, f32[32,128]{1,0:T(8,128)S(1)}, f32[32,128,1]{1,0,2:T(8,128)S...) while((s32[]{:T(128)}, f32[3,32,128]{2,1,0:T(8,128)S(1)}, ...), condition=%wide.region_19.20_spmd.clone.clone, body=%wide.region_15.0_spmd.sunk.clone.clone.sunk | while | flops 22130688 | bytes 13484231 | solution.py:138
  804.5 4.2 fusion.221
  953.8 34.7 %all_to_all.5 = f32[128,7,128]{2,1,0:T(8,128)S(1)} all-to-all(f32[128,7,128]{2,1,0:T(8,128)S(1)} %copy.13), channel_id=1, replica_groups=mesh['gx'=8,'gy'=8,'gz'=4] {'gx','gy'}, dimensions={0} | all-to-all | bytes 917504 | tf_op jit(solution)/shard_map/all_to_all | solution.py:203
  (1022 shorter events, 831.6 us)
Async XLA Ops:
  3.0 6.0 collective-permute-start.1
  5.0 5.2 collective-permute-start
  10.3 5.9 collective-permute-start.3
  11.6 6.1 collective-permute-start.2
  17.8 6.0 collective-permute-start.5
  20.8 6.0 collective-permute-start.4
  27.8 118.1 %copy-start.2 = (s32[32,1]{0,1:T(1,128)S(1)}, s32[32,1]{0,1:T(1,128)}, u32[]{:S(2)}) copy-start(s32[32,1]{0,1:T(1,128)} %param.21) | copy-start | bytes 388
  141.6 4.5 collective-permute-start.7
  143.5 5.6 collective-permute-start.6
  149.2 6.5 collective-permute-start.9
  150.5 6.7 collective-permute-start.8
  157.5 6.5 collective-permute-start.11
  159.4 6.5 collective-permute-start.10
  168.2 310.1 %copy-start.1 = (f32[3]{0:T(128)S(1)}, f32[3]{0:T(128)}, u32[]{:S(2)}) copy-start(f32[3]{0:T(128)} %constant.290.clone.1) | copy-start | bytes 40
  478.5 4.5 collective-permute-start.13
  480.4 5.2 collective-permute-start.12
  485.7 6.2 collective-permute-start.15
  487.0 6.5 collective-permute-start.14
  493.6 6.2 collective-permute-start.17
  495.5 6.0 collective-permute-start.16
  616.2 4.4 collective-permute-start.19
  618.2 5.6 collective-permute-start.18
  623.8 6.5 collective-permute-start.21
  625.1 6.7 collective-permute-start.20
  632.1 6.5 collective-permute-start.23
  634.1 6.5 collective-permute-start.22
  953.0 36.4 %copy-start = (f32[32,128]{1,0:T(8,128)}, f32[32,128]{1,0:T(8,128)S(1)}, u32[]{:S(2)}) copy-start(f32[32,128]{1,0:T(8,128)S(1)} %get-tuple-element.1276) | copy-start | bytes 49156
where the time goes:
time: 1000 us; the launch traced here: 989 us
  other arithmetic  771 us (77%)
  local copies, waits for them, and re-layouts  84.3 us (8%)
  starting transfers between devices  65.2 us (7%)
  blocking collectives  34.7 us (3%)
  waiting for transfers between devices  26.1 us (3%)
    reduce_sum x54, other arithmetic, accel_pair(): jnp.sum((own_vel[:, :, :, None] - near_vel[:, :, None, :]) * relative, ax...  225 us
    reduce_sum x54, other arithmetic, accel_pair(): return -jnp.sum(weight[None] * relative, axis=3)  207 us
    reduce_sum x54, other arithmetic, geometry(): dist_sq = jnp.sum(relative * relative, axis=0)  112 us
    mul x54, other arithmetic, accel_pair(): near_mass[:, None, :]  101 us
    add x108, local copies, waits for them, and re-layouts, geometry(): near_pos + shift[:, None, None]  75.5 us
    reduce_sum x54, other arithmetic, density_pair(): return jnp.sum(near_mass[:, None, :] * kernel, axis=2)  70.7 us
    ppermute x12, starting transfers between devices, extended(): before = lax.ppermute(last, axis, up)  43.6 us
    div x54, other arithmetic, pressure_term(): return STIFF * (seventh - 1.0) / (density * density)  40 us
  transfers between devices with their start and end apart: 24, of which 16 were waited for; matrix products, arithmetic and copies ran while one was open for 0% of the time, Pallas kernels for 0%

commit v1 on v0

v1 whole, which is shorter than its diff:
```python
import functools
import math

import jax
import jax.numpy as jnp
import numpy as np
from jax import lax
from jax.experimental import pallas as pl
from jax.experimental.pallas import tpu as pltpu
from jax.sharding import PartitionSpec as P

SUBSTEPS = 2
ALPHA = 21.0 / (16.0 * math.pi)
STIFF = 0.002
RHO_REST = 0.15
FLOOR = 0.05
VISCOSITY = 0.1
GRAVITY = 1.0
TIMESTEP = 0.2

LANES = 128
TINY = 1e-30
DISPLACEMENTS = [(a, b, c) for a in (-1, 0, 1) for b in (-1, 0, 1) for c in (-1, 0, 1)]
ROWS = 29
CHUNK = 8


def pressure_term(density):
    ratio = density * (1.0 / RHO_REST)
    ratio_sq = ratio * ratio
    seventh = ratio_sq * ratio_sq * ratio_sq * ratio
    return STIFF * (seventh - 1.0) / (density * density)


def pack_sources(bins_ref, counts_ref, packed_ref, spot, grid, load):
    _, padded_y, padded_z = grid
    lane = lax.broadcasted_iota(jnp.int32, (8, LANES), 1)
    field = lax.broadcasted_iota(jnp.int32, (8, LANES), 0)
    units = [jnp.where(field == axis, 1.0, 0.0) for axis in range(3)]
    place = jnp.int32(0)
    current = jnp.zeros((8, LANES), jnp.float32)
    for step in DISPLACEMENTS:
        near = spot + (step[0] * padded_y + step[1]) * padded_z + step[2]
        number = counts_ref[near]
        block = load(near)
        for axis in range(3):
            if step[axis] > 0:
                block = block + units[axis]
            elif step[axis] < 0:
                block = block - units[axis]
        offset = lax.bitwise_and(place, LANES - 1)
        row = lax.shift_right_logical(place, 7)
        rolled = pltpu.roll(block, offset, 1)
        current = jnp.where(lane >= offset, rolled, current)
        packed_ref[row] = current
        place = place + number
        crossed = lax.shift_right_logical(place, 7) > row
        rest = jnp.where(lane < offset, rolled, 0.0)
        current = jnp.where(crossed, rest, current)
    row = lax.shift_right_logical(place, 7)
    packed_ref[row] = current
    packed_ref[row + 1] = jnp.zeros((8, LANES), jnp.float32)
    return lax.shift_right_logical(place + (LANES - 1), 7)


def own_spot(number, own, grid):
    own_y, own_z = own[1], own[2]
    _, padded_y, padded_z = grid
    at_x = number // (own_y * own_z)
    at_y = lax.rem(number // own_z, own_y)
    at_z = lax.rem(number, own_z)
    return ((at_x + 1) * padded_y + at_y + 1) * padded_z + at_z + 1


def spread(ref, row, field):
    return jnp.broadcast_to(ref[row, field : field + 1, :], (8, LANES))


def row_sums(ref):
    ones = jnp.ones((8, LANES), jnp.float32)
    return lax.dot_general(
        ones,
        ref[...],
        (((1,), (1,)), ((), ())),
        precision=lax.Precision.HIGHEST,
        preferred_element_type=jnp.float32,
    )


def in_chunks(groups, body):
    chunks = jnp.where(groups > CHUNK, 2, 1)

    def one(index, carry):
        half = jnp.where(chunks == 2, lax.shift_right_logical(groups + 1, 1), groups)
        first = index * half
        size = jnp.where(index == 0, half, groups - half)
        for known in range(1, CHUNK + 1):

            @pl.when(size == known)
            def _():
                body(first, known)

        return carry

    lax.fori_loop(0, chunks, one, 0)


def density_kernel(own, grid, counts_ref, bins_ref, out_ref, packed_ref, wide_ref, sums_ref):
    lane = lax.broadcasted_iota(jnp.int32, (8, LANES), 1)

    def one_bin(number, carry):
        spot = own_spot(number, own, grid)
        mine = counts_ref[spot]
        rows = pack_sources(bins_ref, counts_ref, packed_ref, spot, grid, lambda near: bins_ref[near])
        columns = jnp.transpose(bins_ref[spot])
        for axis in range(3):
            wide_ref[axis] = jnp.broadcast_to(columns[:, axis : axis + 1], (LANES, LANES))
        groups = jnp.minimum(lax.shift_right_logical(mine + 8, 3), LANES // 8)

        def sweep(first, size):
            unroll = 2 if size <= 4 else 1
            at = [pl.ds(pl.multiple_of((first + g) * 8, 8), 8) for g in range(size)]

            def one_row(turn, totals):
                totals = list(totals)
                for part in range(unroll):
                    row = turn * unroll + part
                    near = [spread(packed_ref, row, axis) for axis in range(3)]
                    mass = spread(packed_ref, row, 6)
                    mass5, mass4 = mass * (5.0 * ALPHA), mass * (4.0 * ALPHA)
                    for g in range(size):
                        x = wide_ref[0, at[g], :] - near[0]
                        y = wide_ref[1, at[g], :] - near[1]
                        z = wide_ref[2, at[g], :] - near[2]
                        square = x * x + y * y + z * z
                        square = jnp.maximum(square, TINY)
                        falloff = jnp.maximum(1.0 - square * lax.rsqrt(square), 0.0)
                        second = falloff * falloff
                        totals[g] = totals[g] + (second * second) * (mass5 - mass4 * falloff)
                return tuple(totals)

            totals = lax.fori_loop(
                0,
                (rows + unroll - 1) // unroll,
                one_row,
                tuple(jnp.zeros((8, LANES), jnp.float32) for _ in range(size)),
            )
            for g in range(size):
                sums_ref[at[g], :] = totals[g]

        in_chunks(groups, sweep)
        result = jnp.maximum(row_sums(sums_ref), FLOOR)
        empty = jnp.sum(jnp.where(lane == mine, result, 0.0), axis=1, keepdims=True)
        result = jnp.where(lane <= mine, result, empty)
        out_ref[number] = result
        return carry

    lax.fori_loop(0, own[0] * own[1] * own[2], one_bin, 0)


def accel_kernel(
    own, grid, counts_ref, where_ref, bins_ref, rho_ref, out_ref, packed_ref, term_ref, wide_ref, sums_ref
):
    bins = own[0] * own[1] * own[2]
    lane = lax.broadcasted_iota(jnp.int32, (8, LANES), 1)
    field = lax.broadcasted_iota(jnp.int32, (8, LANES), 0)
    slots = out_ref.shape[0]
    if slots != bins:

        def clear(number, carry):
            out_ref[number] = jnp.zeros((8, LANES), jnp.float32)
            return carry

        lax.fori_loop(0, slots, clear, 0)

    def whole(near):
        return jnp.where(field == 7, jnp.broadcast_to(rho_ref[pl.ds(near, 1), :], (8, LANES)), bins_ref[near])

    def one_bin(number, carry):
        spot = own_spot(number, own, grid)
        mine = counts_ref[spot]
        rows = pack_sources(bins_ref, counts_ref, packed_ref, spot, grid, whole)
        density = jnp.maximum(packed_ref[:, 7, :], FLOOR)
        term_ref[:, 0, :] = pressure_term(density)
        term_ref[:, 1, :] = density * (1.0 / VISCOSITY)
        block = whole(spot)
        my_rho = jnp.broadcast_to(jnp.maximum(rho_ref[pl.ds(spot, 1), :], FLOOR), (8, LANES))
        mixed = jnp.where(field == 6, pressure_term(my_rho), block)
        mixed = jnp.where(field == 7, my_rho * (1.0 / VISCOSITY), mixed)
        columns = jnp.transpose(mixed)
        for each in range(8):
            wide_ref[each] = jnp.broadcast_to(columns[:, each : each + 1], (LANES, LANES))
        groups = lax.shift_right_logical(mine + 7, 3)

        def sweep(first, size):
            unroll = 2 if size <= 4 else 1
            at = [pl.ds(pl.multiple_of((first + g) * 8, 8), 8) for g in range(size)]

            def one_row(turn, totals):
                totals = list(totals)
                for part in range(unroll):
                    row = turn * unroll + part
                    near = [spread(packed_ref, row, each) for each in range(7)]
                    near_term = spread(term_ref, row, 0)
                    near_rho = spread(term_ref, row, 1)
                    for g in range(size):
                        x = wide_ref[0, at[g], :] - near[0]
                        y = wide_ref[1, at[g], :] - near[1]
                        z = wide_ref[2, at[g], :] - near[2]
                        square = x * x + y * y + z * z
                        approach = (
                            (wide_ref[3, at[g], :] - near[3]) * x
                            + (wide_ref[4, at[g], :] - near[4]) * y
                            + (wide_ref[5, at[g], :] - near[5]) * z
                        )
                        approach = jnp.minimum(approach, 0.0)
                        below = (square + 0.0025) * (wide_ref[7, at[g], :] + near_rho)
                        viscous = approach / below
                        square = jnp.maximum(square, TINY)
                        falloff = jnp.maximum(1.0 - square * lax.rsqrt(square), 0.0)
                        third = falloff * falloff * falloff
                        weight = ((wide_ref[6, at[g], :] + near_term) - viscous) * (near[6] * third)
                        totals[3 * g] = totals[3 * g] + weight * x
                        totals[3 * g + 1] = totals[3 * g + 1] + weight * y
                        totals[3 * g + 2] = totals[3 * g + 2] + weight * z
                return tuple(totals)

            totals = lax.fori_loop(
                0,
                (rows + unroll - 1) // unroll,
                one_row,
                tuple(jnp.zeros((8, LANES), jnp.float32) for _ in range(3 * size)),
            )
            for g in range(size):
                for axis in range(3):
                    sums_ref[axis, at[g], :] = totals[3 * g + axis]

        in_chunks(groups, sweep)
        pulled = [row_sums(sums_ref.at[axis]) * (10.0 * ALPHA) for axis in range(3)]
        pulled[2] = pulled[2] - GRAVITY
        accel = jnp.zeros((8, LANES), jnp.float32)
        for axis in range(3):
            accel = jnp.where(field == axis, pulled[axis], accel)
        accel = jnp.where(lane < mine, accel, 0.0)
        before = bins_ref[spot]
        velocity = pltpu.roll(before, 5, 0) + TIMESTEP * accel
        position = before + (0.5 * TIMESTEP) * velocity
        after = jnp.where(field < 3, position, jnp.where(field < 6, pltpu.roll(velocity, 3, 0), before))
        after = jnp.where(field == 7, 0.0, after)
        if slots != bins:
            after = jnp.where(field < 3, after * 2.0, after)
        out_ref[where_ref[number]] = after
        return carry

    lax.fori_loop(0, bins, one_bin, 0)


VMEM_SPEC = pl.BlockSpec(memory_space=pltpu.VMEM)
SMEM_SPEC = pl.BlockSpec(memory_space=pltpu.SMEM)


def density_of(counts, bins, own, grid):
    number = own[0] * own[1] * own[2]
    out = pl.pallas_call(
        functools.partial(density_kernel, own, grid),
        out_shape=jax.ShapeDtypeStruct((number, 8, LANES), jnp.float32),
        in_specs=[SMEM_SPEC, VMEM_SPEC],
        out_specs=VMEM_SPEC,
        scratch_shapes=[
            pltpu.VMEM((ROWS, 8, LANES), jnp.float32),
            pltpu.VMEM((3, LANES, LANES), jnp.float32),
            pltpu.VMEM((LANES, LANES), jnp.float32),
        ],
        compiler_params=pltpu.CompilerParams(vmem_limit_bytes=32 * 1024 * 1024),
        name="density",
    )(counts, bins)
    return out[:, 0, :]


def moved(counts, where_to, bins, rho, own, grid, slots):
    return pl.pallas_call(
        functools.partial(accel_kernel, own, grid),
        out_shape=jax.ShapeDtypeStruct((slots, 8, LANES), jnp.float32),
        in_specs=[SMEM_SPEC, SMEM_SPEC, VMEM_SPEC, VMEM_SPEC],
        out_specs=VMEM_SPEC,
        scratch_shapes=[
            pltpu.VMEM((ROWS, 8, LANES), jnp.float32),
            pltpu.VMEM((ROWS, 8, LANES), jnp.float32),
            pltpu.VMEM((8, LANES, LANES), jnp.float32),
            pltpu.VMEM((3, LANES, LANES), jnp.float32),
        ],
        compiler_params=pltpu.CompilerParams(vmem_limit_bytes=32 * 1024 * 1024),
        name="accel",
    )(counts, where_to, bins, rho)


def extended(value):
    for dim, axis in enumerate(("gx", "gy", "gz")):
        devices, length = (lax.axis_size(axis), value.shape[dim])
        up = [(i, i + 1) for i in range(devices - 1)]
        down = [(j, i) for i, j in up]
        last = lax.slice_in_dim(value, length - 1, length, axis=dim)
        initial = lax.slice_in_dim(value, 0, 1, axis=dim)
        before = lax.ppermute(last, axis, up)
        after = lax.ppermute(initial, axis, down)
        value = jnp.concatenate([before, value, after], axis=dim)
    return value


def local(offsets, velocity, mass, counts, owner):
    own = counts.shape
    grid = tuple(extent + 2 for extent in own)
    bins = own[0] * own[1] * own[2]
    padded = grid[0] * grid[1] * grid[2]
    slot_ids = jnp.arange(LANES, dtype=jnp.int32)
    alive = slot_ids < counts[..., None]
    fields = jnp.concatenate([offsets * 0.5, velocity, mass[None], jnp.zeros_like(mass)[None]], 0)
    states = jnp.where(alive[..., None, :], jnp.transpose(fields, (1, 2, 3, 0, 4)), 0.0)
    layers = lax.axis_size("gx") * lax.axis_size("gy")
    capacity = max(2, 2 * bins // layers)
    target = owner[:, 0]
    earlier = np.tril(np.ones((bins, bins), bool), -1)
    rank = jnp.sum(((target[:, None] == target[None, :]) & earlier).astype(jnp.int32), axis=1)
    where_to = target * capacity + rank
    in_order = jnp.arange(bins, dtype=jnp.int32)
    near_counts = None
    for substep in range(SUBSTEPS):
        near = extended(states).reshape(padded, 8, LANES)
        if near_counts is None:
            near_counts = jnp.sum((near[:, 6, :] > 0.0).astype(jnp.int32), axis=1)
        density = density_of(near_counts, near, own, grid)
        near_rho = extended(density.reshape(own + (LANES,))).reshape(padded, LANES)
        last = substep == SUBSTEPS - 1
        states = moved(
            near_counts,
            where_to if last else in_order,
            near,
            near_rho,
            own,
            grid,
            layers * capacity if last else bins,
        )
        if not last:
            states = states.reshape(own + (8, LANES))
    arrived = lax.all_to_all(states, ("gx", "gy"), split_axis=0, concat_axis=0, tiled=True)
    return (arrived[:, :7, :], density.reshape(own + (LANES,)))


def solution(mesh):
    placed = (
        P(None, "gx", "gy", "gz", None),
        P(None, "gx", "gy", "gz", None),
        P("gx", "gy", "gz", None),
        P("gx", "gy", "gz"),
        P(("gx", "gy", "gz"), None),
    )
    return jax.shard_map(
        local,
        mesh=mesh,
        in_specs=placed,
        out_specs=(P(("gx", "gy", "gz"), None, None), P("gx", "gy", "gz", None)),
        check_vma=False,
    )
```

time: 1000 us -> 355 us (0.35); the launches traced: 989 us -> 357 us
  other arithmetic: 771 us -> 4.47 us
  Pallas kernels: 0 us -> 194 us
  local copies, waits for them, and re-layouts: 84.3 us -> 1.46 us
  waiting for transfers between devices: 26.1 us -> 41.8 us
  starting transfers between devices: 65.2 us -> 77.6 us
    reduce_sum x217 -> x2, other arithmetic: 615 us -> 2.82 us  [the longest x1 2.64 us: local(): near_counts = jnp.sum((near[:, 6, :] > 0.0).astype(jnp.int32), axis=1)]
    pallas_call x0 -> x4, Pallas kernels: none -> 194 us  [the longest x2 119 us: moved(): pl.pallas_call(functools.partial(accel_kernel, own, grid), out_shape=jax....]
    mul x58 -> x1, other arithmetic: 103 us -> 0.84 us  [local(): offsets * 0.5]
    add x108 -> x0, local copies, waits for them, and re-layouts: 75.5 us -> none  [geometry(): near_pos + shift[:, None, None]]
    div x54 -> x0, other arithmetic: 40 us -> none  [pressure_term(): return STIFF * (seventh - 1.0) / (density * density)]
    ppermute x12, waiting for transfers between devices: 1.32 us -> 38.4 us  [extended(): after = lax.ppermute(initial, axis, down)]
    ppermute x12, waiting for transfers between devices: 24.8 us -> 3.41 us  [extended(): before = lax.ppermute(last, axis, up)]
    ppermute x12, starting transfers between devices: 43.6 us -> 54.8 us  [extended(): before = lax.ppermute(last, axis, up)]
where the time goes in v1:
time: 355 us; the launch traced here: 357 us
  Pallas kernels  194 us (55%)
  starting transfers between devices  77.6 us (22%)
  waiting for transfers between devices  41.8 us (12%)
  blocking collectives  36.4 us (10%)
  other arithmetic  4.47 us (1%)
    pallas_call x2, Pallas kernels, moved(): pl.pallas_call(functools.partial(accel_kernel, own, grid), out_shape=jax....  119 us
    pallas_call x2, Pallas kernels, density_of(): pl.pallas_call(functools.partial(density_kernel, own, grid), out_shape=ja...  74.9 us
    ppermute x12, starting transfers between devices, extended(): before = lax.ppermute(last, axis, up)  54.8 us
    ppermute x12, waiting for transfers between devices, extended(): after = lax.ppermute(initial, axis, down)  38.4 us
    all_to_all x1, blocking collectives, local(): lax.all_to_all(states, ('gx', 'gy'), split_axis=0, concat_axis=0, tiled=T...  36.4 us
    ppermute x12, starting transfers between devices, extended(): after = lax.ppermute(initial, axis, down)  22.8 us
  transfers between devices with their start and end apart: 24, of which 16 were waited for; matrix products, arithmetic and copies ran while one was open for 0% of the time, Pallas kernels for 0%

profile of v1, /device:TPU:10, one launch (start us, length us, event | category | flops | bytes accessed | tf_op | source)
XLA Modules:
  0.0 356.6 jit_solution(6784541125784392875)
XLA Ops:
  1.8 1.9 collective-permute-start
  3.7 3.6 %collective-permute-start.1 = (f32[1,4,4,8,128]{4,2,1,0,3:T(4,128)S(1)}, f32[1,4,4,8,128]{4,2,1,0,3:T(4,128)S(1)}, u32[]{:S(2)}, u32[]{:S(2)}) collective-permute-start(f32[1,4,4,8,128]{4,2,1,0,3:T(4,128)S(1)} %get-tuple-element.23), channel_id=1, source_target_pairs={{32,0},{64,32},{96,64},{128,96},{160,128},{192,160},{224,192},{33,... | collective-permute-start | bytes 196616 | tf_op jit(solution)/shard_map/ppermute | solution.py:305
  9.3 3.8 %collective-permute-start.2 = (f32[4,1,4,8,128]{4,2,1,0,3:T(4,128)S(1)}, f32[4,1,4,8,128]{4,2,1,0,3:T(4,128)S(1)}, u32[]{:S(2)}, u32[]{:S(2)}) collective-permute-start(f32[4,1,4,8,128]{4,2,1,0,3:T(4,128)S(1)} %get-tuple-element.14), channel_id=1, source_target_pairs={{0,4},{4,8},{8,12},{12,16},{16,20},{20,24},{24,28},{1,5},{5,9},{9,... | collective-permute-start | bytes 196616 | tf_op jit(solution)/shard_map/ppermute | solution.py:304
  15.0 4.4 %collective-permute-done.3 = f32[4,1,4,8,128]{4,2,1,0,3:T(4,128)S(1)} collective-permute-done((f32[4,1,4,8,128]{4,2,1,0,3:T(4,128)S(1)}, f32[4,1,4,8,128]{4,2,1,0,3:T(4,128)S(1)}, u32[]{:S(2)}, u32[]{:S(2)}) %collective-permute-start.3) | collective-permute-done | bytes 65568 | tf_op jit(solution)/shard_map/ppermute | solution.py:305
  19.5 3.4 collective-permute-start.4
  22.9 2.4 collective-permute-start.5
  26.5 3.1 collective-permute-done.5
  30.3 2.6 fusion.1.counts_ref
  32.9 37.4 %density.2 = f32[32,8,128]{2,1,0:T(8,128)S(1)} custom-call(s32[144]{0:T(256)S(1)} %fusion.1.counts_ref, f32[144,8,128]{2,1,0:T(8,128)S(1)} %bitcast.19), custom_call_target="tpu_custom_call" | custom-call | tf_op jit(solution)/shard_map/density/pallas_call | solution.py:264
  70.4 4.1 %collective-permute-start.6 = (f32[1,4,4,128]{3,2,1,0:T(4,128)S(1)}, f32[1,4,4,128]{3,2,1,0:T(4,128)S(1)}, u32[]{:S(2)}, u32[]{:S(2)}) collective-permute-start(f32[1,4,4,128]{3,2,1,0:T(4,128)S(1)} %bitcast.39), channel_id=1, source_target_pairs={{0,32},{32,64},{64,96},{96,128},{128,160},{160,192},{192,224},{1,3... | collective-permute-start | bytes 24584 | tf_op jit(solution)/shard_map/ppermute | solution.py:304
  74.5 1.9 collective-permute-start.7
  77.8 6.2 %collective-permute-start.8 = (f32[4,1,4,128]{3,2,1,0:T(4,128)S(1)}, f32[4,1,4,128]{3,2,1,0:T(4,128)S(1)}, u32[]{:S(2)}, u32[]{:S(2)}) collective-permute-start(f32[4,1,4,128]{3,2,1,0:T(4,128)S(1)} %get-tuple-element.30), channel_id=1, source_target_pairs={{0,4},{4,8},{8,12},{12,16},{16,20},{20,24},{24,28},{1,5},{5,9},{9,... | collective-permute-start | bytes 24584 | tf_op jit(solution)/shard_map/ppermute | solution.py:304
  85.4 4.3 %collective-permute-done.9 = f32[4,1,4,128]{3,2,1,0:T(4,128)S(1)} collective-permute-done((f32[4,1,4,128]{3,2,1,0:T(4,128)S(1)}, f32[4,1,4,128]{3,2,1,0:T(4,128)S(1)}, u32[]{:S(2)}, u32[]{:S(2)}) %collective-permute-start.9) | collective-permute-done | bytes 8224 | tf_op jit(solution)/shard_map/ppermute | solution.py:305
  89.7 4.7 %collective-permute-start.10 = (f32[4,6,1,128]{3,2,1,0:T(1,128)S(1)}, f32[4,6,1,128]{3,2,1,0:T(1,128)S(1)}, u32[]{:S(2)}, u32[]{:S(2)}) collective-permute-start(f32[4,6,1,128]{3,2,1,0:T(1,128)S(1)} %get-tuple-element.26), channel_id=1, source_target_pairs={{0,1},{1,2},{2,3},{4,5},{5,6},{6,7},{8,9},{9,10},{10,11},{12,13},{... | collective-permute-start | bytes 36872 | tf_op jit(solution)/shard_map/ppermute | solution.py:304
  94.4 1.9 collective-permute-start.11
  96.4 3.6 %collective-permute-done.11 = f32[4,6,1,128]{3,2,1,0:T(1,128)S(1)} collective-permute-done((f32[4,6,1,128]{3,2,1,0:T(1,128)S(1)}, f32[4,6,1,128]{3,2,1,0:T(1,128)S(1)}, u32[]{:S(2)}, u32[]{:S(2)}) %collective-permute-start.11) | collective-permute-done | bytes 12320 | tf_op jit(solution)/shard_map/ppermute | solution.py:305
  100.1 59.1 %accel.2 = f32[32,8,128]{2,1,0:T(8,128)S(1)} custom-call(s32[144]{0:T(256)S(1)} %fusion.1.counts_ref, s32[32]{0:T(128)S(1)} %iota.8.where_ref, f32[144,8,128]{2,1,0:T(8,128)S(1)} %bitcast.20, f32[144,128]{1,0:T(8,128)S(1)} %reshape.34.rho_ref), custom_call_target="tpu_custom_call" | custom-call | tf_op jit(solution)/shard_map/accel/pallas_call | solution.py:281
  159.2 7.0 %collective-permute-start.12 = (f32[1,4,4,8,128]{4,3,2,1,0:T(8,128)S(1)}, f32[1,4,4,8,128]{4,3,2,1,0:T(8,128)S(1)}, u32[]{:S(2)}, u32[]{:S(2)}) collective-permute-start(f32[1,4,4,8,128]{4,3,2,1,0:T(8,128)S(1)} %bitcast.35), channel_id=1, source_target_pairs={{0,32},{32,64},{64,96},{96,128},{128,160},{160,192},{192,224},{1,3... | collective-permute-start | bytes 196616 | tf_op jit(solution)/shard_map/ppermute | solution.py:304
  166.2 1.9 collective-permute-start.13
  170.0 6.6 %collective-permute-start.14 = (f32[4,1,4,8,128]{4,3,2,1,0:T(8,128)S(1)}, f32[4,1,4,8,128]{4,3,2,1,0:T(8,128)S(1)}, u32[]{:S(2)}, u32[]{:S(2)}) collective-permute-start(f32[4,1,4,8,128]{4,3,2,1,0:T(8,128)S(1)} %get-tuple-element.12), channel_id=1, source_target_pairs={{0,4},{4,8},{8,12},{12,16},{16,20},{20,24},{24,28},{1,5},{5,9},{9,... | collective-permute-start | bytes 196616 | tf_op jit(solution)/shard_map/ppermute | solution.py:304
  178.5 4.5 %collective-permute-done.15 = f32[4,1,4,8,128]{4,3,2,1,0:T(8,128)S(1)} collective-permute-done((f32[4,1,4,8,128]{4,3,2,1,0:T(8,128)S(1)}, f32[4,1,4,8,128]{4,3,2,1,0:T(8,128)S(1)}, u32[]{:S(2)}, u32[]{:S(2)}) %collective-permute-start.15) | collective-permute-done | bytes 65568 | tf_op jit(solution)/shard_map/ppermute | solution.py:305
  183.0 4.0 %collective-permute-start.16 = (f32[4,6,1,8,128]{4,3,2,1,0:T(8,128)S(1)}, f32[4,6,1,8,128]{4,3,2,1,0:T(8,128)S(1)}, u32[]{:S(2)}, u32[]{:S(2)}) collective-permute-start(f32[4,6,1,8,128]{4,3,2,1,0:T(8,128)S(1)} %get-tuple-element.8), channel_id=1, source_target_pairs={{0,1},{1,2},{2,3},{4,5},{5,6},{6,7},{8,9},{9,10},{10,11},{12,13},{... | collective-permute-start | bytes 294920 | tf_op jit(solution)/shard_map/ppermute | solution.py:304
  189.9 4.4 %collective-permute-done.17 = f32[4,6,1,8,128]{4,3,2,1,0:T(8,128)S(1)} collective-permute-done((f32[4,6,1,8,128]{4,3,2,1,0:T(8,128)S(1)}, f32[4,6,1,8,128]{4,3,2,1,0:T(8,128)S(1)}, u32[]{:S(2)}, u32[]{:S(2)}) %collective-permute-start.17) | collective-permute-done | bytes 98336 | tf_op jit(solution)/shard_map/ppermute | solution.py:305
  194.3 37.4 %density.3 = f32[32,8,128]{2,1,0:T(8,128)S(1)} custom-call(s32[144]{0:T(256)S(1)} %fusion.1.counts_ref, f32[144,8,128]{2,1,0:T(8,128)S(1)} %bitcast.21), custom_call_target="tpu_custom_call" | custom-call | tf_op jit(solution)/shard_map/density/pallas_call | solution.py:264
  231.8 4.9 %collective-permute-start.18 = (f32[1,4,4,128]{3,2,1,0:T(4,128)S(1)}, f32[1,4,4,128]{3,2,1,0:T(4,128)S(1)}, u32[]{:S(2)}, u32[]{:S(2)}) collective-permute-start(f32[1,4,4,128]{3,2,1,0:T(4,128)S(1)} %bitcast.40), channel_id=1, source_target_pairs={{0,32},{32,64},{64,96},{96,128},{128,160},{160,192},{192,224},{1,3... | collective-permute-start | bytes 24584 | tf_op jit(solution)/shard_map/ppermute | solution.py:304
  236.7 1.9 collective-permute-start.19
  240.0 3.4 collective-permute-start.20
  245.0 4.0 %collective-permute-done.21 = f32[4,1,4,128]{3,2,1,0:T(4,128)S(1)} collective-permute-done((f32[4,1,4,128]{3,2,1,0:T(4,128)S(1)}, f32[4,1,4,128]{3,2,1,0:T(4,128)S(1)}, u32[]{:S(2)}, u32[]{:S(2)}) %collective-permute-start.21) | collective-permute-done | bytes 8224 | tf_op jit(solution)/shard_map/ppermute | solution.py:305
  249.0 4.8 %collective-permute-start.22 = (f32[4,6,1,128]{3,2,1,0:T(1,128)S(1)}, f32[4,6,1,128]{3,2,1,0:T(1,128)S(1)}, u32[]{:S(2)}, u32[]{:S(2)}) collective-permute-start(f32[4,6,1,128]{3,2,1,0:T(1,128)S(1)} %get-tuple-element.24), channel_id=1, source_target_pairs={{0,1},{1,2},{2,3},{4,5},{5,6},{6,7},{8,9},{9,10},{10,11},{12,13},{... | collective-permute-start | bytes 36872 | tf_op jit(solution)/shard_map/ppermute | solution.py:304
  255.8 3.6 %collective-permute-done.23 = f32[4,6,1,128]{3,2,1,0:T(1,128)S(1)} collective-permute-done((f32[4,6,1,128]{3,2,1,0:T(1,128)S(1)}, f32[4,6,1,128]{3,2,1,0:T(1,128)S(1)}, u32[]{:S(2)}, u32[]{:S(2)}) %collective-permute-start.23) | collective-permute-done | bytes 12320 | tf_op jit(solution)/shard_map/ppermute | solution.py:305
  259.5 59.8 %accel.3 = f32[128,8,128]{2,1,0:T(8,128)S(1)} custom-call(s32[144]{0:T(256)S(1)} %fusion.1.counts_ref, s32[32]{0:T(128)S(1)} %multiply_add_fusion.where_ref, f32[144,8,128]{2,1,0:T(8,128)S(1)} %bitcast.22, f32[144,128]{1,0:T(8,128)S(1)} %reshape.37.rho_ref), custom_call_target="tpu_custom_call" | custom-call | tf_op jit(solution)/shard_map/accel/pallas_call | solution.py:281
  319.3 36.4 %all_to_all.5 = f32[128,8,128]{2,1,0:T(8,128)S(1)} all-to-all(f32[128,8,128]{2,1,0:T(8,128)S(1)} %accel.3), channel_id=1, replica_groups=mesh['gx'=8,'gy'=8,'gz'=4] {'gx','gy'}, dimensions={0} | all-to-all | bytes 1048576 | tf_op jit(solution)/shard_map/all_to_all | solution.py:345
  (63 shorter events, 22.1 us)
Async XLA Ops:
  0.6 0.9 copy-start.3
  0.6 1.0 copy-start.1
  0.7 1.0 copy-start.2
  1.8 5.6 %collective-permute-start = (f32[1,4,4,8,128]{4,2,1,0,3:T(4,128)S(1)}, f32[1,4,4,8,128]{4,2,1,0,3:T(4,128)S(1)}, u32[]{:S(2)}, u32[]{:S(2)}) collective-permute-start(f32[1,4,4,8,128]{4,2,1,0,3:T(4,128)S(1)} %get-tuple-element.22), channel_id=1, source_target_pairs={{0,32},{32,64},{64,96},{96,128},{128,160},{160,192},{192,224},{1,3... | collective-permute-start | bytes 196616 | tf_op jit(solution)/shard_map/ppermute | solution.py:304
  3.7 5.5 %collective-permute-start.1 = (f32[1,4,4,8,128]{4,2,1,0,3:T(4,128)S(1)}, f32[1,4,4,8,128]{4,2,1,0,3:T(4,128)S(1)}, u32[]{:S(2)}, u32[]{:S(2)}) collective-permute-start(f32[1,4,4,8,128]{4,2,1,0,3:T(4,128)S(1)} %get-tuple-element.23), channel_id=1, source_target_pairs={{32,0},{64,32},{96,64},{128,96},{160,128},{192,160},{224,192},{33,... | collective-permute-start | bytes 196616 | tf_op jit(solution)/shard_map/ppermute | solution.py:305
  9.3 5.7 %collective-permute-start.2 = (f32[4,1,4,8,128]{4,2,1,0,3:T(4,128)S(1)}, f32[4,1,4,8,128]{4,2,1,0,3:T(4,128)S(1)}, u32[]{:S(2)}, u32[]{:S(2)}) collective-permute-start(f32[4,1,4,8,128]{4,2,1,0,3:T(4,128)S(1)} %get-tuple-element.14), channel_id=1, source_target_pairs={{0,4},{4,8},{8,12},{12,16},{16,20},{20,24},{24,28},{1,5},{5,9},{9,... | collective-permute-start | bytes 196616 | tf_op jit(solution)/shard_map/ppermute | solution.py:304
  13.1 6.2 %collective-permute-start.3 = (f32[4,1,4,8,128]{4,2,1,0,3:T(4,128)S(1)}, f32[4,1,4,8,128]{4,2,1,0,3:T(4,128)S(1)}, u32[]{:S(2)}, u32[]{:S(2)}) collective-permute-start(f32[4,1,4,8,128]{4,2,1,0,3:T(4,128)S(1)} %get-tuple-element.15), channel_id=1, source_target_pairs={{4,0},{8,4},{12,8},{16,12},{20,16},{24,20},{28,24},{5,1},{9,5},{13... | collective-permute-start | bytes 196616 | tf_op jit(solution)/shard_map/ppermute | solution.py:305
  19.5 7.0 %collective-permute-start.4 = (f32[4,6,1,8,128]{4,2,1,0,3:T(1,128)S(1)}, f32[4,6,1,8,128]{4,2,1,0,3:T(1,128)S(1)}, u32[]{:S(2)}, u32[]{:S(2)}) collective-permute-start(f32[4,6,1,8,128]{4,2,1,0,3:T(1,128)S(1)} %get-tuple-element.10), channel_id=1, source_target_pairs={{0,1},{1,2},{2,3},{4,5},{5,6},{6,7},{8,9},{9,10},{10,11},{12,13},{... | collective-permute-start | bytes 294920 | tf_op jit(solution)/shard_map/ppermute | solution.py:304
  22.9 6.8 %collective-permute-start.5 = (f32[4,6,1,8,128]{4,2,1,0,3:T(1,128)S(1)}, f32[4,6,1,8,128]{4,2,1,0,3:T(1,128)S(1)}, u32[]{:S(2)}, u32[]{:S(2)}) collective-permute-start(f32[4,6,1,8,128]{4,2,1,0,3:T(1,128)S(1)} %get-tuple-element.11), channel_id=1, source_target_pairs={{1,0},{2,1},{3,2},{5,4},{6,5},{7,6},{9,8},{10,9},{11,10},{13,12},{... | collective-permute-start | bytes 294920 | tf_op jit(solution)/shard_map/ppermute | solution.py:305
  70.4 6.1 %collective-permute-start.6 = (f32[1,4,4,128]{3,2,1,0:T(4,128)S(1)}, f32[1,4,4,128]{3,2,1,0:T(4,128)S(1)}, u32[]{:S(2)}, u32[]{:S(2)}) collective-permute-start(f32[1,4,4,128]{3,2,1,0:T(4,128)S(1)} %bitcast.39), channel_id=1, source_target_pairs={{0,32},{32,64},{64,96},{96,128},{128,160},{160,192},{192,224},{1,3... | collective-permute-start | bytes 24584 | tf_op jit(solution)/shard_map/ppermute | solution.py:304
  74.5 3.3 collective-permute-start.7
  77.8 7.5 %collective-permute-start.8 = (f32[4,1,4,128]{3,2,1,0:T(4,128)S(1)}, f32[4,1,4,128]{3,2,1,0:T(4,128)S(1)}, u32[]{:S(2)}, u32[]{:S(2)}) collective-permute-start(f32[4,1,4,128]{3,2,1,0:T(4,128)S(1)} %get-tuple-element.30), channel_id=1, source_target_pairs={{0,4},{4,8},{8,12},{12,16},{16,20},{20,24},{24,28},{1,5},{5,9},{9,... | collective-permute-start | bytes 24584 | tf_op jit(solution)/shard_map/ppermute | solution.py:304
  84.0 5.7 %collective-permute-start.9 = (f32[4,1,4,128]{3,2,1,0:T(4,128)S(1)}, f32[4,1,4,128]{3,2,1,0:T(4,128)S(1)}, u32[]{:S(2)}, u32[]{:S(2)}) collective-permute-start(f32[4,1,4,128]{3,2,1,0:T(4,128)S(1)} %get-tuple-element.31), channel_id=1, source_target_pairs={{4,0},{8,4},{12,8},{16,12},{20,16},{24,20},{28,24},{5,1},{9,5},{13... | collective-permute-start | bytes 24584 | tf_op jit(solution)/shard_map/ppermute | solution.py:305
  89.7 6.6 %collective-permute-start.10 = (f32[4,6,1,128]{3,2,1,0:T(1,128)S(1)}, f32[4,6,1,128]{3,2,1,0:T(1,128)S(1)}, u32[]{:S(2)}, u32[]{:S(2)}) collective-permute-start(f32[4,6,1,128]{3,2,1,0:T(1,128)S(1)} %get-tuple-element.26), channel_id=1, source_target_pairs={{0,1},{1,2},{2,3},{4,5},{5,6},{6,7},{8,9},{9,10},{10,11},{12,13},{... | collective-permute-start | bytes 36872 | tf_op jit(solution)/shard_map/ppermute | solution.py:304
  94.4 5.6 %collective-permute-start.11 = (f32[4,6,1,128]{3,2,1,0:T(1,128)S(1)}, f32[4,6,1,128]{3,2,1,0:T(1,128)S(1)}, u32[]{:S(2)}, u32[]{:S(2)}) collective-permute-start(f32[4,6,1,128]{3,2,1,0:T(1,128)S(1)} %get-tuple-element.27), channel_id=1, source_target_pairs={{1,0},{2,1},{3,2},{5,4},{6,5},{7,6},{9,8},{10,9},{11,10},{13,12},{... | collective-permute-start | bytes 36872 | tf_op jit(solution)/shard_map/ppermute | solution.py:305
  159.2 8.9 %collective-permute-start.12 = (f32[1,4,4,8,128]{4,3,2,1,0:T(8,128)S(1)}, f32[1,4,4,8,128]{4,3,2,1,0:T(8,128)S(1)}, u32[]{:S(2)}, u32[]{:S(2)}) collective-permute-start(f32[1,4,4,8,128]{4,3,2,1,0:T(8,128)S(1)} %bitcast.35), channel_id=1, source_target_pairs={{0,32},{32,64},{64,96},{96,128},{128,160},{160,192},{192,224},{1,3... | collective-permute-start | bytes 196616 | tf_op jit(solution)/shard_map/ppermute | solution.py:304
  166.2 3.8 %collective-permute-start.13 = (f32[1,4,4,8,128]{4,3,2,1,0:T(8,128)S(1)}, f32[1,4,4,8,128]{4,3,2,1,0:T(8,128)S(1)}, u32[]{:S(2)}, u32[]{:S(2)}) collective-permute-start(f32[1,4,4,8,128]{4,3,2,1,0:T(8,128)S(1)} %bitcast.34), channel_id=1, source_target_pairs={{32,0},{64,32},{96,64},{128,96},{160,128},{192,160},{224,192},{33,... | collective-permute-start | bytes 196616 | tf_op jit(solution)/shard_map/ppermute | solution.py:305
  170.0 8.5 %collective-permute-start.14 = (f32[4,1,4,8,128]{4,3,2,1,0:T(8,128)S(1)}, f32[4,1,4,8,128]{4,3,2,1,0:T(8,128)S(1)}, u32[]{:S(2)}, u32[]{:S(2)}) collective-permute-start(f32[4,1,4,8,128]{4,3,2,1,0:T(8,128)S(1)} %get-tuple-element.12), channel_id=1, source_target_pairs={{0,4},{4,8},{8,12},{12,16},{16,20},{20,24},{24,28},{1,5},{5,9},{9,... | collective-permute-start | bytes 196616 | tf_op jit(solution)/shard_map/ppermute | solution.py:304
  176.6 6.4 %collective-permute-start.15 = (f32[4,1,4,8,128]{4,3,2,1,0:T(8,128)S(1)}, f32[4,1,4,8,128]{4,3,2,1,0:T(8,128)S(1)}, u32[]{:S(2)}, u32[]{:S(2)}) collective-permute-start(f32[4,1,4,8,128]{4,3,2,1,0:T(8,128)S(1)} %get-tuple-element.13), channel_id=1, source_target_pairs={{4,0},{8,4},{12,8},{16,12},{20,16},{24,20},{28,24},{5,1},{9,5},{13... | collective-permute-start | bytes 196616 | tf_op jit(solution)/shard_map/ppermute | solution.py:305
  183.0 6.9 %collective-permute-start.16 = (f32[4,6,1,8,128]{4,3,2,1,0:T(8,128)S(1)}, f32[4,6,1,8,128]{4,3,2,1,0:T(8,128)S(1)}, u32[]{:S(2)}, u32[]{:S(2)}) collective-permute-start(f32[4,6,1,8,128]{4,3,2,1,0:T(8,128)S(1)} %get-tuple-element.8), channel_id=1, source_target_pairs={{0,1},{1,2},{2,3},{4,5},{5,6},{6,7},{8,9},{9,10},{10,11},{12,13},{... | collective-permute-start | bytes 294920 | tf_op jit(solution)/shard_map/ppermute | solution.py:304
  187.0 7.3 %collective-permute-start.17 = (f32[4,6,1,8,128]{4,3,2,1,0:T(8,128)S(1)}, f32[4,6,1,8,128]{4,3,2,1,0:T(8,128)S(1)}, u32[]{:S(2)}, u32[]{:S(2)}) collective-permute-start(f32[4,6,1,8,128]{4,3,2,1,0:T(8,128)S(1)} %get-tuple-element.9), channel_id=1, source_target_pairs={{1,0},{2,1},{3,2},{5,4},{6,5},{7,6},{9,8},{10,9},{11,10},{13,12},{... | collective-permute-start | bytes 294920 | tf_op jit(solution)/shard_map/ppermute | solution.py:305
  231.8 6.9 %collective-permute-start.18 = (f32[1,4,4,128]{3,2,1,0:T(4,128)S(1)}, f32[1,4,4,128]{3,2,1,0:T(4,128)S(1)}, u32[]{:S(2)}, u32[]{:S(2)}) collective-permute-start(f32[1,4,4,128]{3,2,1,0:T(4,128)S(1)} %bitcast.40), channel_id=1, source_target_pairs={{0,32},{32,64},{64,96},{96,128},{128,160},{160,192},{192,224},{1,3... | collective-permute-start | bytes 24584 | tf_op jit(solution)/shard_map/ppermute | solution.py:304
  236.7 3.3 collective-permute-start.19
  238.7 20.8 %copy-start = (f32[32,1,128]{2,1,0:T(1,128)}, f32[32,1,128]{2,1,0:T(1,128)S(1)}, u32[]{:S(2)}) copy-start(f32[32,1,128]{2,1,0:T(1,128)S(1)} %slice.149) | copy-start | bytes 49156
  240.0 4.7 %copy-start.4 = (pred[32,32]{1,0:T(32,128)(4,1)S(1)}, pred[32,32]{1,0:T(32,128)(4,1)}, u32[]{:S(2)}) copy-start(pred[32,32]{1,0:T(32,128)(4,1)} %constant.3.clone) | copy-start | bytes 3076
  240.0 4.9 %collective-permute-start.20 = (f32[4,1,4,128]{3,2,1,0:T(4,128)S(1)}, f32[4,1,4,128]{3,2,1,0:T(4,128)S(1)}, u32[]{:S(2)}, u32[]{:S(2)}) collective-permute-start(f32[4,1,4,128]{3,2,1,0:T(4,128)S(1)} %get-tuple-element.28), channel_id=1, source_target_pairs={{0,4},{4,8},{8,12},{12,16},{16,20},{20,24},{24,28},{1,5},{5,9},{9,... | collective-permute-start | bytes 24584 | tf_op jit(solution)/shard_map/ppermute | solution.py:304
  243.4 1.3 copy-start.5
  243.5 5.5 %collective-permute-start.21 = (f32[4,1,4,128]{3,2,1,0:T(4,128)S(1)}, f32[4,1,4,128]{3,2,1,0:T(4,128)S(1)}, u32[]{:S(2)}, u32[]{:S(2)}) collective-permute-start(f32[4,1,4,128]{3,2,1,0:T(4,128)S(1)} %get-tuple-element.29), channel_id=1, source_target_pairs={{4,0},{8,4},{12,8},{16,12},{20,16},{24,20},{28,24},{5,1},{9,5},{13... | collective-permute-start | bytes 24584 | tf_op jit(solution)/shard_map/ppermute | solution.py:305
  249.0 6.8 %collective-permute-start.22 = (f32[4,6,1,128]{3,2,1,0:T(1,128)S(1)}, f32[4,6,1,128]{3,2,1,0:T(1,128)S(1)}, u32[]{:S(2)}, u32[]{:S(2)}) collective-permute-start(f32[4,6,1,128]{3,2,1,0:T(1,128)S(1)} %get-tuple-element.24), channel_id=1, source_target_pairs={{0,1},{1,2},{2,3},{4,5},{5,6},{6,7},{8,9},{9,10},{10,11},{12,13},{... | collective-permute-start | bytes 36872 | tf_op jit(solution)/shard_map/ppermute | solution.py:304
  253.9 5.6 %collective-permute-start.23 = (f32[4,6,1,128]{3,2,1,0:T(1,128)S(1)}, f32[4,6,1,128]{3,2,1,0:T(1,128)S(1)}, u32[]{:S(2)}, u32[]{:S(2)}) collective-permute-start(f32[4,6,1,128]{3,2,1,0:T(1,128)S(1)} %get-tuple-element.25), channel_id=1, source_target_pairs={{1,0},{2,1},{3,2},{5,4},{6,5},{7,6},{9,8},{10,9},{11,10},{13,12},{... | collective-permute-start | bytes 36872 | tf_op jit(solution)/shard_map/ppermute | solution.py:305

commit v2 on v1

v2 whole, which is shorter than its diff:
```python
import functools
import math

import jax
import jax.numpy as jnp
import numpy as np
from jax import lax
from jax.experimental import pallas as pl
from jax.experimental.pallas import tpu as pltpu
from jax.sharding import PartitionSpec as P

SUBSTEPS = 2
ALPHA = 21.0 / (16.0 * math.pi)
STIFF = 0.002
RHO_REST = 0.15
FLOOR = 0.05
VISCOSITY = 0.1
GRAVITY = 1.0
TIMESTEP = 0.2

LANES = 128
TINY = 1e-30
DISPLACEMENTS = [(a, b, c) for a in (-1, 0, 1) for b in (-1, 0, 1) for c in (-1, 0, 1)]
ROWS = 32
UNROLL_MOST = 4
CHUNK = 8
VMEM_LIMIT = 48 * 1024 * 1024


def pressure_term(density):
    ratio = density * (1.0 / RHO_REST)
    ratio_sq = ratio * ratio
    seventh = ratio_sq * ratio_sq * ratio_sq * ratio
    return STIFF * (seventh - 1.0) / (density * density)


def pack_sources(counts_ref, packed_ref, number, spot, grid, load):
    _, padded_y, padded_z = grid
    lane = lax.broadcasted_iota(jnp.int32, (8, LANES), 1)
    field = lax.broadcasted_iota(jnp.int32, (8, LANES), 0)
    units = [jnp.where(field == axis, 1.0, 0.0) for axis in range(3)]
    place = jnp.int32(0)
    current = jnp.zeros((8, LANES), jnp.float32)
    for step in DISPLACEMENTS:
        near = spot + (step[0] * padded_y + step[1]) * padded_z + step[2]
        block = load(near)
        for axis in range(3):
            if step[axis] > 0:
                block = block + units[axis]
            elif step[axis] < 0:
                block = block - units[axis]
        offset = lax.bitwise_and(place, LANES - 1)
        row = lax.shift_right_logical(place, 7)
        rolled = pltpu.roll(block, offset, 1)
        current = jnp.where(lane >= offset, rolled, current)
        packed_ref[number, row] = current
        place = place + counts_ref[near]
        crossed = lax.shift_right_logical(place, 7) > row
        rest = jnp.where(lane < offset, rolled, 0.0)
        current = jnp.where(crossed, rest, current)
    row = lax.shift_right_logical(place, 7)
    packed_ref[number, row] = jnp.where(lane < lax.bitwise_and(place, LANES - 1), current, 0.0)
    for more in range(1, UNROLL_MOST):
        packed_ref[number, row + more] = jnp.zeros((8, LANES), jnp.float32)
    return lax.shift_right_logical(place + (LANES - 1), 7)


def spread_columns(wide_ref, number, block, fields, groups):
    columns = jnp.transpose(block)
    half = LANES // 2

    def fill(first):
        for each in range(fields):
            wide_ref[number, each, pl.ds(first, half), :] = jnp.broadcast_to(
                columns[first : first + half, each : each + 1], (half, LANES)
            )

    fill(0)

    @pl.when(groups > half // 8)
    def _():
        fill(half)


def own_spot(number, own, grid):
    own_y, own_z = own[1], own[2]
    _, padded_y, padded_z = grid
    at_x = number // (own_y * own_z)
    at_y = lax.rem(number // own_z, own_y)
    at_z = lax.rem(number, own_z)
    return ((at_x + 1) * padded_y + at_y + 1) * padded_z + at_z + 1


def spread(ref, number, row, field):
    return jnp.broadcast_to(ref[number, row, field : field + 1, :], (8, LANES))


def row_sums(sums):
    lane = lax.broadcasted_iota(jnp.int32, (LANES, LANES), 1)
    row = lax.broadcasted_iota(jnp.int32, (LANES, LANES), 0)
    total = jnp.broadcast_to(jnp.sum(sums, axis=1, keepdims=True), (LANES, LANES))
    total = jnp.sum(jnp.where(lane == row, total, 0.0).reshape(LANES // 8, 8, LANES), axis=0)
    return jnp.broadcast_to(jnp.sum(total, axis=0, keepdims=True), (8, LANES))


def by_size(size, least, most, body):
    if least == most:
        body(least)
        return
    middle = (least + most) // 2

    @pl.when(size <= middle)
    def _():
        by_size(size, least, middle, body)

    @pl.when(size > middle)
    def _():
        by_size(size, middle + 1, most, body)


def each_bin(bins, body):
    def turn(index, carry):
        for part in range(4):
            body(index * 4 + part)
        return carry

    lax.fori_loop(0, bins // 4, turn, 0)


def density_kernel(own, grid, counts_ref, bins_ref, out_ref, packed_ref, wide_ref, sums_ref, rows_ref):
    bins = own[0] * own[1] * own[2]
    lane = lax.broadcasted_iota(jnp.int32, (8, LANES), 1)

    def groups_of(spot):
        return jnp.minimum(lax.shift_right_logical(counts_ref[spot] + 8, 3), LANES // 8)

    def prepare(number):
        spot = own_spot(number, own, grid)
        rows_ref[number] = pack_sources(
            counts_ref, packed_ref, number, spot, grid, lambda near: bins_ref[near]
        )
        spread_columns(wide_ref, number, bins_ref[spot], 3, groups_of(spot))

    each_bin(bins, prepare)

    def one_bin(number, carry):
        rows = rows_ref[number]

        def sweep(size):
            unroll = 2 if size > 7 else 4

            def one_row(turn, totals):
                totals = list(totals)
                for part in range(unroll):
                    row = turn * unroll + part
                    near = [spread(packed_ref, number, row, axis) for axis in range(3)]
                    mass = spread(packed_ref, number, row, 6)
                    mass5, mass4 = mass * (5.0 * ALPHA), mass * (4.0 * ALPHA)
                    for g in range(size):
                        at = pl.ds(g * 8, 8)
                        x = wide_ref[number, 0, at, :] - near[0]
                        y = wide_ref[number, 1, at, :] - near[1]
                        z = wide_ref[number, 2, at, :] - near[2]
                        square = x * x + y * y + z * z
                        square = jnp.maximum(square, TINY)
                        falloff = jnp.maximum(1.0 - square * lax.rsqrt(square), 0.0)
                        second = falloff * falloff
                        totals[g] = totals[g] + (second * second) * (mass5 - mass4 * falloff)
                return tuple(totals)

            totals = lax.fori_loop(
                0,
                lax.shift_right_logical(rows + unroll - 1, 1 if unroll == 2 else 2),
                one_row,
                tuple(jnp.zeros((8, LANES), jnp.float32) for _ in range(size)),
            )
            for g in range(size):
                sums_ref[number, pl.ds(g * 8, 8), :] = totals[g]

        by_size(groups_of(own_spot(number, own, grid)), 1, LANES // 8, sweep)
        return carry

    lax.fori_loop(0, bins, one_bin, 0)

    def finish(number):
        mine = counts_ref[own_spot(number, own, grid)]
        result = jnp.maximum(row_sums(sums_ref[number]), FLOOR)
        empty = jnp.sum(jnp.where(lane == mine, result, 0.0), axis=1, keepdims=True)
        result = jnp.where(lane <= mine, result, empty)
        out_ref[pl.ds(number, 1), :] = result[0:1]

    each_bin(bins, finish)


def accel_kernel(
    own,
    grid,
    counts_ref,
    where_ref,
    bins_ref,
    rho_ref,
    out_ref,
    packed_ref,
    term_ref,
    wide_ref,
    sums_ref,
    rows_ref,
):
    bins = own[0] * own[1] * own[2]
    lane = lax.broadcasted_iota(jnp.int32, (8, LANES), 1)
    field = lax.broadcasted_iota(jnp.int32, (8, LANES), 0)
    slots = out_ref.shape[0]
    if slots != bins:

        def clear(turn, carry):
            out_ref[pl.ds(turn * 8, 8)] = jnp.zeros((8, 8, LANES), jnp.float32)
            return carry

        lax.fori_loop(0, slots // 8, clear, 0)

    def groups_of(spot):
        return lax.shift_right_logical(counts_ref[spot] + 7, 3)

    def whole(near):
        return jnp.where(field == 7, jnp.broadcast_to(rho_ref[pl.ds(near, 1), :], (8, LANES)), bins_ref[near])

    def prepare(number):
        spot = own_spot(number, own, grid)
        rows_ref[number] = pack_sources(counts_ref, packed_ref, number, spot, grid, whole)
        density = jnp.maximum(packed_ref[number, :, 7, :], FLOOR)
        term_ref[number, 0] = pressure_term(density)
        term_ref[number, 1] = density * (1.0 / VISCOSITY)
        my_rho = jnp.broadcast_to(jnp.maximum(rho_ref[pl.ds(spot, 1), :], FLOOR), (8, LANES))
        mixed = jnp.where(field == 6, pressure_term(my_rho), bins_ref[spot])
        mixed = jnp.where(field == 7, my_rho * (1.0 / VISCOSITY), mixed)
        spread_columns(wide_ref, number, mixed, 8, groups_of(spot))

    each_bin(bins, prepare)

    def one_bin(number, carry):
        rows = rows_ref[number]
        groups = groups_of(own_spot(number, own, grid))

        def chunk(index, carry):
            half = jnp.where(groups > CHUNK, lax.shift_right_logical(groups + 1, 1), groups)
            first = index * half
            length = jnp.where(index == 0, half, groups - half)

            def sweep(size):
                unroll = 2 if size > 2 else 4
                at = [pl.ds(pl.multiple_of((first + g) * 8, 8), 8) for g in range(size)]

                def one_row(turn, totals):
                    totals = list(totals)
                    for part in range(unroll):
                        row = turn * unroll + part
                        near = [spread(packed_ref, number, row, each) for each in range(7)]
                        near_term = jnp.broadcast_to(term_ref[number, 0, pl.ds(row, 1), :], (8, LANES))
                        near_rho = jnp.broadcast_to(term_ref[number, 1, pl.ds(row, 1), :], (8, LANES))
                        for g in range(size):
                            x = wide_ref[number, 0, at[g], :] - near[0]
                            y = wide_ref[number, 1, at[g], :] - near[1]
                            z = wide_ref[number, 2, at[g], :] - near[2]
                            square = x * x + y * y + z * z
                            approach = (
                                (wide_ref[number, 3, at[g], :] - near[3]) * x
                                + (wide_ref[number, 4, at[g], :] - near[4]) * y
                                + (wide_ref[number, 5, at[g], :] - near[5]) * z
                            )
                            approach = jnp.minimum(approach, 0.0)
                            below = (square + 0.0025) * (wide_ref[number, 7, at[g], :] + near_rho)
                            viscous = approach / below
                            square = jnp.maximum(square, TINY)
                            falloff = jnp.maximum(1.0 - square * lax.rsqrt(square), 0.0)
                            third = falloff * falloff * falloff
                            weight = ((wide_ref[number, 6, at[g], :] + near_term) - viscous) * (near[6] * third)
                            totals[3 * g] = totals[3 * g] + weight * x
                            totals[3 * g + 1] = totals[3 * g + 1] + weight * y
                            totals[3 * g + 2] = totals[3 * g + 2] + weight * z
                    return tuple(totals)

                totals = lax.fori_loop(
                    0,
                    lax.shift_right_logical(rows + unroll - 1, 1 if unroll == 2 else 2),
                    one_row,
                    tuple(jnp.zeros((8, LANES), jnp.float32) for _ in range(3 * size)),
                )
                for g in range(size):
                    for axis in range(3):
                        sums_ref[number, axis, at[g], :] = totals[3 * g + axis]

            by_size(length, 1, CHUNK, sweep)
            return carry

        lax.fori_loop(0, jnp.where(groups > CHUNK, 2, 1), chunk, 0)
        return carry

    lax.fori_loop(0, bins, one_bin, 0)

    def finish(number):
        spot = own_spot(number, own, grid)
        pulled = [row_sums(sums_ref[number, axis]) * (10.0 * ALPHA) for axis in range(3)]
        pulled[2] = pulled[2] - GRAVITY
        accel = jnp.zeros((8, LANES), jnp.float32)
        for axis in range(3):
            accel = jnp.where(field == axis, pulled[axis], accel)
        accel = jnp.where(lane < counts_ref[spot], accel, 0.0)
        before = bins_ref[spot]
        velocity = pltpu.roll(before, 5, 0) + TIMESTEP * accel
        position = before + (0.5 * TIMESTEP) * velocity
        after = jnp.where(field < 3, position, jnp.where(field < 6, pltpu.roll(velocity, 3, 0), before))
        after = jnp.where(field == 7, 0.0, after)
        if slots != bins:
            after = jnp.where(field < 3, after * 2.0, after)
        out_ref[where_ref[number]] = after

    each_bin(bins, finish)


VMEM_SPEC = pl.BlockSpec(memory_space=pltpu.VMEM)
SMEM_SPEC = pl.BlockSpec(memory_space=pltpu.SMEM)


def density_of(counts, bins, own, grid):
    number = own[0] * own[1] * own[2]
    return pl.pallas_call(
        functools.partial(density_kernel, own, grid),
        out_shape=jax.ShapeDtypeStruct((number, LANES), jnp.float32),
        in_specs=[SMEM_SPEC, VMEM_SPEC],
        out_specs=VMEM_SPEC,
        scratch_shapes=[
            pltpu.VMEM((number, ROWS, 8, LANES), jnp.float32),
            pltpu.VMEM((number, 3, LANES, LANES), jnp.float32),
            pltpu.VMEM((number, LANES, LANES), jnp.float32),
            pltpu.SMEM((number,), jnp.int32),
        ],
        compiler_params=pltpu.CompilerParams(vmem_limit_bytes=VMEM_LIMIT),
        name="density",
    )(counts, bins)


def moved(counts, where_to, bins, rho, own, grid, slots):
    number = own[0] * own[1] * own[2]
    return pl.pallas_call(
        functools.partial(accel_kernel, own, grid),
        out_shape=jax.ShapeDtypeStruct((slots, 8, LANES), jnp.float32),
        in_specs=[SMEM_SPEC, SMEM_SPEC, VMEM_SPEC, VMEM_SPEC],
        out_specs=VMEM_SPEC,
        scratch_shapes=[
            pltpu.VMEM((number, ROWS, 8, LANES), jnp.float32),
            pltpu.VMEM((number, 2, ROWS, LANES), jnp.float32),
            pltpu.VMEM((number, 8, LANES, LANES), jnp.float32),
            pltpu.VMEM((number, 3, LANES, LANES), jnp.float32),
            pltpu.SMEM((number,), jnp.int32),
        ],
        compiler_params=pltpu.CompilerParams(vmem_limit_bytes=VMEM_LIMIT),
        name="accel",
    )(counts, where_to, bins, rho)


def extended(value):
    for dim, axis in enumerate(("gx", "gy", "gz")):
        devices, length = (lax.axis_size(axis), value.shape[dim])
        up = [(i, (i + 1) % devices) for i in range(devices)]
        down = [(j, i) for i, j in up]
        last = lax.slice_in_dim(value, length - 1, length, axis=dim)
        initial = lax.slice_in_dim(value, 0, 1, axis=dim)
        before = lax.ppermute(last, axis, up)
        after = lax.ppermute(initial, axis, down)
        value = jnp.concatenate([before, value, after], axis=dim)
    return value


def inside(grid):
    result = jnp.ones(grid, bool)
    for dim, axis in enumerate(("gx", "gy", "gz")):
        place = lax.broadcasted_iota(jnp.int32, grid, dim)
        device, last = lax.axis_index(axis), lax.axis_size(axis) - 1
        outside = ((place == 0) & (device == 0)) | ((place == grid[dim] - 1) & (device == last))
        result = result & ~outside
    return result


def local(offsets, velocity, mass, counts, owner):
    own = counts.shape
    grid = tuple(extent + 2 for extent in own)
    bins = own[0] * own[1] * own[2]
    padded = grid[0] * grid[1] * grid[2]
    slot_ids = jnp.arange(LANES, dtype=jnp.int32)
    alive = slot_ids < counts[..., None]
    fields = jnp.concatenate([offsets * 0.5, velocity, mass[None], jnp.zeros_like(mass)[None]], 0)
    states = jnp.where(alive[..., None, :], jnp.transpose(fields, (1, 2, 3, 0, 4)), 0.0)
    layers = lax.axis_size("gx") * lax.axis_size("gy")
    capacity = max(2, 2 * bins // layers)
    target = owner[:, 0]
    earlier = np.tril(np.ones((bins, bins), bool), -1)
    rank = jnp.sum(((target[:, None] == target[None, :]) & earlier).astype(jnp.int32), axis=1)
    where_to = target * capacity + rank
    in_order = jnp.arange(bins, dtype=jnp.int32)
    near_counts = None
    for substep in range(SUBSTEPS):
        near = extended(states).reshape(padded, 8, LANES)
        if near_counts is None:
            occupied = (near[:, 6, :] > 0.0) & inside(grid).reshape(padded, 1)
            near_counts = jnp.sum(occupied.astype(jnp.int32), axis=1)
        density = density_of(near_counts, near, own, grid)
        near_rho = extended(density.reshape(own + (LANES,))).reshape(padded, LANES)
        last = substep == SUBSTEPS - 1
        states = moved(
            near_counts,
            where_to if last else in_order,
            near,
            near_rho,
            own,
            grid,
            layers * capacity if last else bins,
        )
        if not last:
            states = states.reshape(own + (8, LANES))
    arrived = lax.all_to_all(states, ("gx", "gy"), split_axis=0, concat_axis=0, tiled=True)
    return (arrived[:, :7, :], density.reshape(own + (LANES,)))


def solution(mesh):
    placed = (
        P(None, "gx", "gy", "gz", None),
        P(None, "gx", "gy", "gz", None),
        P("gx", "gy", "gz", None),
        P("gx", "gy", "gz"),
        P(("gx", "gy", "gz"), None),
    )
    return jax.shard_map(
        local,
        mesh=mesh,
        in_specs=placed,
        out_specs=(P(("gx", "gy", "gz"), None, None), P("gx", "gy", "gz", None)),
        check_vma=False,
    )
```

time: 355 us -> 254 us (0.72); the launches traced: 357 us -> 249 us
  Pallas kernels: 194 us -> 136 us
  starting transfers between devices: 77.6 us -> 43.9 us
  waiting for transfers between devices: 41.8 us -> 33.3 us
  blocking collectives: 36.4 us -> 29.8 us
    pallas_call x2, Pallas kernels: 119 us -> 85.3 us  [moved(): pl.pallas_call(functools.partial(accel_kernel, own, grid), out_shape=jax....]
    ppermute x12, waiting for transfers between devices: 38.4 us -> 12.1 us  [extended(): after = lax.ppermute(initial, axis, down)]
    ppermute x12, starting transfers between devices: 54.8 us -> 29.6 us  [extended(): before = lax.ppermute(last, axis, up)]
    pallas_call x2, Pallas kernels: 74.9 us -> 51 us  [density_of(): pl.pallas_call(functools.partial(density_kernel, own, grid), out_shape=ja...]
    ppermute x12, waiting for transfers between devices: 3.41 us -> 21.2 us  [extended(): before = lax.ppermute(last, axis, up)]
    ppermute x12, starting transfers between devices: 22.8 us -> 14.3 us  [extended(): after = lax.ppermute(initial, axis, down)]
    all_to_all x1, blocking collectives: 36.4 us -> 29.8 us  [local(): lax.all_to_all(states, ('gx', 'gy'), split_axis=0, concat_axis=0, tiled=T...]
  transfers between devices with their start and end apart: 24 -> 24, of which waited for: 16 -> 19; matrix products, arithmetic and copies ran while one was open for 0% -> 0% of each run, Pallas kernels for 0% -> 0%
where the time goes in v2:
time: 254 us; the launch traced here: 249 us
  Pallas kernels  136 us (54%)
  starting transfers between devices  43.9 us (17%)
  waiting for transfers between devices  33.3 us (13%)
  blocking collectives  29.8 us (12%)
  local copies, waits for them, and re-layouts  2.88 us (1%)
    pallas_call x2, Pallas kernels, moved(): pl.pallas_call(functools.partial(accel_kernel, own, grid), out_shape=jax....  85.3 us
    pallas_call x2, Pallas kernels, density_of(): pl.pallas_call(functools.partial(density_kernel, own, grid), out_shape=ja...  51 us
    all_to_all x1, blocking collectives, local(): lax.all_to_all(states, ('gx', 'gy'), split_axis=0, concat_axis=0, tiled=T...  29.8 us
    ppermute x12, starting transfers between devices, extended(): before = lax.ppermute(last, axis, up)  29.6 us
    ppermute x12, waiting for transfers between devices, extended(): before = lax.ppermute(last, axis, up)  21.2 us
    ppermute x12, starting transfers between devices, extended(): after = lax.ppermute(initial, axis, down)  14.3 us
    ppermute x12, waiting for transfers between devices, extended(): after = lax.ppermute(initial, axis, down)  12.1 us
  transfers between devices with their start and end apart: 24, of which 19 were waited for; matrix products, arithmetic and copies ran while one was open for 0% of the time, Pallas kernels for 0%

profile of v2, /device:TPU:10, one launch (start us, length us, event | category | flops | bytes accessed | tf_op | source)
XLA Modules:
  0.0 249.2 jit_solution(6853333336144801772)
XLA Ops:
  1.8 1.7 collective-permute-start.1
  3.5 1.9 collective-permute-done
  5.5 2.0 collective-permute-start.2
  7.5 4.0 %collective-permute-start.3 = (f32[4,1,4,8,128]{4,2,1,0,3:T(4,128)S(1)}, f32[4,1,4,8,128]{4,2,1,0,3:T(4,128)S(1)}, u32[]{:S(2)}, u32[]{:S(2)}) collective-permute-start(f32[4,1,4,8,128]{4,2,1,0,3:T(4,128)S(1)} %get-tuple-element.15), channel_id=1, source_target_pairs={{4,0},{8,4},{12,8},{16,12},{20,16},{24,20},{28,24},{0,28},{5,1},{9... | collective-permute-start | bytes 196616 | tf_op jit(solution)/shard_map/ppermute | solution.py:369
  11.6 2.1 collective-permute-done.2
  13.9 1.6 collective-permute-start.4
  16.2 3.3 %collective-permute-done.4 = f32[4,6,1,8,128]{4,2,1,0,3:T(1,128)S(1)} collective-permute-done((f32[4,6,1,8,128]{4,2,1,0,3:T(1,128)S(1)}, f32[4,6,1,8,128]{4,2,1,0,3:T(1,128)S(1)}, u32[]{:S(2)}, u32[]{:S(2)}) %collective-permute-start.4) | collective-permute-done | bytes 98336 | tf_op jit(solution)/shard_map/ppermute | solution.py:368
  21.6 25.2 %density.2 = f32[32,128]{1,0:T(8,128)S(1)} custom-call(s32[144]{0:T(256)S(1)} %convert_reduce_fusion.counts_ref, f32[144,8,128]{2,1,0:T(8,128)S(1)} %bitcast.23), custom_call_target="tpu_custom_call" | custom-call | tf_op jit(solution)/shard_map/density/pallas_call | solution.py:326
  46.8 1.7 collective-permute-start.7
  49.9 2.0 collective-permute-start.8
  51.9 2.0 collective-permute-start.9
  53.9 1.5 collective-permute-done.8
  55.6 3.5 %collective-permute-start.10 = (f32[4,6,1,128]{3,2,1,0:T(1,128)S(1)}, f32[4,6,1,128]{3,2,1,0:T(1,128)S(1)}, u32[]{:S(2)}, u32[]{:S(2)}) collective-permute-start(f32[4,6,1,128]{3,2,1,0:T(1,128)S(1)} %get-tuple-element.22), channel_id=1, source_target_pairs={{0,1},{1,2},{2,3},{3,0},{4,5},{5,6},{6,7},{7,4},{8,9},{9,10},{10,1... | collective-permute-start | bytes 36872 | tf_op jit(solution)/shard_map/ppermute | solution.py:368
  59.1 1.4 collective-permute-done.10
  60.5 2.3 collective-permute-done.11
  62.9 42.6 %accel.2 = f32[32,8,128]{2,1,0:T(8,128)S(1)} custom-call(s32[144]{0:T(256)S(1)} %convert_reduce_fusion.counts_ref, s32[32]{0:T(128)S(1)} %iota.39.where_ref, f32[144,8,128]{2,1,0:T(8,128)S(1)} %bitcast.24, f32[144,128]{1,0:T(8,128)S(1)} %reshape.102.rho_ref), custom_call_target="tpu_custom_call" | custom-call | tf_op jit(solution)/shard_map/accel/pallas_call | solution.py:344
  105.5 1.7 collective-permute-start.13
  107.2 1.9 collective-permute-done.12
  109.2 9.4 %collective-permute-start.14 = (f32[4,1,4,8,128]{4,3,2,1,0:T(8,128)S(1)}, f32[4,1,4,8,128]{4,3,2,1,0:T(8,128)S(1)}, u32[]{:S(2)}, u32[]{:S(2)}) collective-permute-start(f32[4,1,4,8,128]{4,3,2,1,0:T(8,128)S(1)} %get-tuple-element.12), channel_id=1, source_target_pairs={{0,4},{4,8},{8,12},{12,16},{16,20},{20,24},{24,28},{28,0},{1,5},{5... | collective-permute-start | bytes 196616 | tf_op jit(solution)/shard_map/ppermute | solution.py:368
  118.6 1.9 collective-permute-done.14
  120.5 2.4 collective-permute-done.15
  122.9 2.8 %collective-permute-start.16 = (f32[4,6,1,8,128]{4,3,2,1,0:T(8,128)S(1)}, f32[4,6,1,8,128]{4,3,2,1,0:T(8,128)S(1)}, u32[]{:S(2)}, u32[]{:S(2)}) collective-permute-start(f32[4,6,1,8,128]{4,3,2,1,0:T(8,128)S(1)} %get-tuple-element.8), channel_id=1, source_target_pairs={{0,1},{1,2},{2,3},{3,0},{4,5},{5,6},{6,7},{7,4},{8,9},{9,10},{10,1... | collective-permute-start | bytes 294920 | tf_op jit(solution)/shard_map/ppermute | solution.py:368
  125.6 2.2 collective-permute-done.16
  127.9 2.4 collective-permute-done.17
  130.3 25.8 %density.3 = f32[32,128]{1,0:T(8,128)} custom-call(s32[144]{0:T(256)S(1)} %convert_reduce_fusion.counts_ref, f32[144,8,128]{2,1,0:T(8,128)S(1)} %bitcast.25), custom_call_target="tpu_custom_call" | custom-call | tf_op jit(solution)/shard_map/density/pallas_call | solution.py:326
  156.9 1.7 collective-permute-start.19
  160.0 7.0 %collective-permute-start.20 = (f32[4,1,4,128]{3,2,1,0:T(4,128)S(1)}, f32[4,1,4,128]{3,2,1,0:T(4,128)S(1)}, u32[]{:S(2)}, u32[]{:S(2)}) collective-permute-start(f32[4,1,4,128]{3,2,1,0:T(4,128)S(1)} %get-tuple-element.24), channel_id=1, source_target_pairs={{0,4},{4,8},{8,12},{12,16},{16,20},{20,24},{24,28},{28,0},{1,5},{5... | collective-permute-start | bytes 24584 | tf_op jit(solution)/shard_map/ppermute | solution.py:368
  168.4 2.3 collective-permute-done.21
  170.7 1.4 collective-permute-start.22
  172.8 1.7 collective-permute-done.22
  175.8 42.7 %accel.3 = f32[128,8,128]{2,1,0:T(8,128)S(1)} custom-call(s32[144]{0:T(256)S(1)} %convert_reduce_fusion.counts_ref, s32[32]{0:T(128)S(1)} %multiply_add_fusion.where_ref, f32[144,8,128]{2,1,0:T(8,128)S(1)} %bitcast.26, f32[144,128]{1,0:T(8,128)S(1)} %reshape.106.rho_ref), custom_call_target="tpu_custom_call" | custom-call | tf_op jit(solution)/shard_map/accel/pallas_call | solution.py:344
  218.5 29.8 %all_to_all.5 = f32[128,8,128]{2,1,0:T(8,128)S(1)} all-to-all(f32[128,8,128]{2,1,0:T(8,128)S(1)} %accel.3), channel_id=1, replica_groups=mesh['gx'=8,'gy'=8,'gz'=4] {'gx','gy'}, dimensions={0} | all-to-all | bytes 1048576 | tf_op jit(solution)/shard_map/all_to_all | solution.py:420
  (66 shorter events, 12.3 us)
Async XLA Ops:
  0.6 0.9 copy-start.3
  0.6 1.0 copy-start.1
  0.7 1.0 copy-start.2
  1.8 3.7 %collective-permute-start = (f32[1,4,4,8,128]{4,2,1,0,3:T(4,128)S(1)}, f32[1,4,4,8,128]{4,2,1,0,3:T(4,128)S(1)}, u32[]{:S(2)}, u32[]{:S(2)}) collective-permute-start(f32[1,4,4,8,128]{4,2,1,0,3:T(4,128)S(1)} %get-tuple-element.18), channel_id=1, source_target_pairs={{0,32},{32,64},{64,96},{96,128},{128,160},{160,192},{192,224},{224... | collective-permute-start | bytes 196616 | tf_op jit(solution)/shard_map/ppermute | solution.py:368
  1.8 3.7 %collective-permute-start.1 = (f32[1,4,4,8,128]{4,2,1,0,3:T(4,128)S(1)}, f32[1,4,4,8,128]{4,2,1,0,3:T(4,128)S(1)}, u32[]{:S(2)}, u32[]{:S(2)}) collective-permute-start(f32[1,4,4,8,128]{4,2,1,0,3:T(4,128)S(1)} %get-tuple-element.19), channel_id=1, source_target_pairs={{32,0},{64,32},{96,64},{128,96},{160,128},{192,160},{224,192},{0,2... | collective-permute-start | bytes 196616 | tf_op jit(solution)/shard_map/ppermute | solution.py:369
  5.5 8.2 %collective-permute-start.2 = (f32[4,1,4,8,128]{4,2,1,0,3:T(4,128)S(1)}, f32[4,1,4,8,128]{4,2,1,0,3:T(4,128)S(1)}, u32[]{:S(2)}, u32[]{:S(2)}) collective-permute-start(f32[4,1,4,8,128]{4,2,1,0,3:T(4,128)S(1)} %get-tuple-element.14), channel_id=1, source_target_pairs={{0,4},{4,8},{8,12},{12,16},{16,20},{20,24},{24,28},{28,0},{1,5},{5... | collective-permute-start | bytes 196616 | tf_op jit(solution)/shard_map/ppermute | solution.py:368
  7.5 6.2 %collective-permute-start.3 = (f32[4,1,4,8,128]{4,2,1,0,3:T(4,128)S(1)}, f32[4,1,4,8,128]{4,2,1,0,3:T(4,128)S(1)}, u32[]{:S(2)}, u32[]{:S(2)}) collective-permute-start(f32[4,1,4,8,128]{4,2,1,0,3:T(4,128)S(1)} %get-tuple-element.15), channel_id=1, source_target_pairs={{4,0},{8,4},{12,8},{16,12},{20,16},{24,20},{28,24},{0,28},{5,1},{9... | collective-permute-start | bytes 196616 | tf_op jit(solution)/shard_map/ppermute | solution.py:369
  13.9 5.6 %collective-permute-start.4 = (f32[4,6,1,8,128]{4,2,1,0,3:T(1,128)S(1)}, f32[4,6,1,8,128]{4,2,1,0,3:T(1,128)S(1)}, u32[]{:S(2)}, u32[]{:S(2)}) collective-permute-start(f32[4,6,1,8,128]{4,2,1,0,3:T(1,128)S(1)} %get-tuple-element.10), channel_id=1, source_target_pairs={{0,1},{1,2},{2,3},{3,0},{4,5},{5,6},{6,7},{7,4},{8,9},{9,10},{10,1... | collective-permute-start | bytes 294920 | tf_op jit(solution)/shard_map/ppermute | solution.py:368
  15.4 5.2 %collective-permute-start.5 = (f32[4,6,1,8,128]{4,2,1,0,3:T(1,128)S(1)}, f32[4,6,1,8,128]{4,2,1,0,3:T(1,128)S(1)}, u32[]{:S(2)}, u32[]{:S(2)}) collective-permute-start(f32[4,6,1,8,128]{4,2,1,0,3:T(1,128)S(1)} %get-tuple-element.11), channel_id=1, source_target_pairs={{1,0},{2,1},{3,2},{0,3},{5,4},{6,5},{7,6},{4,7},{9,8},{10,9},{11,1... | collective-permute-start | bytes 294920 | tf_op jit(solution)/shard_map/ppermute | solution.py:369
  46.8 3.1 %collective-permute-start.6 = (f32[1,4,4,128]{3,2,1,0:T(4,128)S(1)}, f32[1,4,4,128]{3,2,1,0:T(4,128)S(1)}, u32[]{:S(2)}, u32[]{:S(2)}) collective-permute-start(f32[1,4,4,128]{3,2,1,0:T(4,128)S(1)} %bitcast.43), channel_id=1, source_target_pairs={{0,32},{32,64},{64,96},{96,128},{128,160},{160,192},{192,224},{224... | collective-permute-start | bytes 24584 | tf_op jit(solution)/shard_map/ppermute | solution.py:368
  46.8 3.1 %collective-permute-start.7 = (f32[1,4,4,128]{3,2,1,0:T(4,128)S(1)}, f32[1,4,4,128]{3,2,1,0:T(4,128)S(1)}, u32[]{:S(2)}, u32[]{:S(2)}) collective-permute-start(f32[1,4,4,128]{3,2,1,0:T(4,128)S(1)} %bitcast.41), channel_id=1, source_target_pairs={{32,0},{64,32},{96,64},{128,96},{160,128},{192,160},{224,192},{0,2... | collective-permute-start | bytes 24584 | tf_op jit(solution)/shard_map/ppermute | solution.py:369
  49.9 5.6 %collective-permute-start.8 = (f32[4,1,4,128]{3,2,1,0:T(4,128)S(1)}, f32[4,1,4,128]{3,2,1,0:T(4,128)S(1)}, u32[]{:S(2)}, u32[]{:S(2)}) collective-permute-start(f32[4,1,4,128]{3,2,1,0:T(4,128)S(1)} %get-tuple-element.26), channel_id=1, source_target_pairs={{0,4},{4,8},{8,12},{12,16},{16,20},{20,24},{24,28},{28,0},{1,5},{5... | collective-permute-start | bytes 24584 | tf_op jit(solution)/shard_map/ppermute | solution.py:368
  51.9 3.7 %collective-permute-start.9 = (f32[4,1,4,128]{3,2,1,0:T(4,128)S(1)}, f32[4,1,4,128]{3,2,1,0:T(4,128)S(1)}, u32[]{:S(2)}, u32[]{:S(2)}) collective-permute-start(f32[4,1,4,128]{3,2,1,0:T(4,128)S(1)} %get-tuple-element.27), channel_id=1, source_target_pairs={{4,0},{8,4},{12,8},{16,12},{20,16},{24,20},{28,24},{0,28},{5,1},{9... | collective-permute-start | bytes 24584 | tf_op jit(solution)/shard_map/ppermute | solution.py:369
  55.6 4.9 %collective-permute-start.10 = (f32[4,6,1,128]{3,2,1,0:T(1,128)S(1)}, f32[4,6,1,128]{3,2,1,0:T(1,128)S(1)}, u32[]{:S(2)}, u32[]{:S(2)}) collective-permute-start(f32[4,6,1,128]{3,2,1,0:T(1,128)S(1)} %get-tuple-element.22), channel_id=1, source_target_pairs={{0,1},{1,2},{2,3},{3,0},{4,5},{5,6},{6,7},{7,4},{8,9},{9,10},{10,1... | collective-permute-start | bytes 36872 | tf_op jit(solution)/shard_map/ppermute | solution.py:368
  59.1 3.7 %collective-permute-start.11 = (f32[4,6,1,128]{3,2,1,0:T(1,128)S(1)}, f32[4,6,1,128]{3,2,1,0:T(1,128)S(1)}, u32[]{:S(2)}, u32[]{:S(2)}) collective-permute-start(f32[4,6,1,128]{3,2,1,0:T(1,128)S(1)} %get-tuple-element.23), channel_id=1, source_target_pairs={{1,0},{2,1},{3,2},{0,3},{5,4},{6,5},{7,6},{4,7},{9,8},{10,9},{11,1... | collective-permute-start | bytes 36872 | tf_op jit(solution)/shard_map/ppermute | solution.py:369
  105.5 3.7 %collective-permute-start.12 = (f32[1,4,4,8,128]{4,3,2,1,0:T(8,128)S(1)}, f32[1,4,4,8,128]{4,3,2,1,0:T(8,128)S(1)}, u32[]{:S(2)}, u32[]{:S(2)}) collective-permute-start(f32[1,4,4,8,128]{4,3,2,1,0:T(8,128)S(1)} %bitcast.39), channel_id=1, source_target_pairs={{0,32},{32,64},{64,96},{96,128},{128,160},{160,192},{192,224},{224... | collective-permute-start | bytes 196616 | tf_op jit(solution)/shard_map/ppermute | solution.py:368
  105.5 3.7 %collective-permute-start.13 = (f32[1,4,4,8,128]{4,3,2,1,0:T(8,128)S(1)}, f32[1,4,4,8,128]{4,3,2,1,0:T(8,128)S(1)}, u32[]{:S(2)}, u32[]{:S(2)}) collective-permute-start(f32[1,4,4,8,128]{4,3,2,1,0:T(8,128)S(1)} %bitcast.38), channel_id=1, source_target_pairs={{32,0},{64,32},{96,64},{128,96},{160,128},{192,160},{224,192},{0,2... | collective-permute-start | bytes 196616 | tf_op jit(solution)/shard_map/ppermute | solution.py:369
  109.2 11.3 %collective-permute-start.14 = (f32[4,1,4,8,128]{4,3,2,1,0:T(8,128)S(1)}, f32[4,1,4,8,128]{4,3,2,1,0:T(8,128)S(1)}, u32[]{:S(2)}, u32[]{:S(2)}) collective-permute-start(f32[4,1,4,8,128]{4,3,2,1,0:T(8,128)S(1)} %get-tuple-element.12), channel_id=1, source_target_pairs={{0,4},{4,8},{8,12},{12,16},{16,20},{20,24},{24,28},{28,0},{1,5},{5... | collective-permute-start | bytes 196616 | tf_op jit(solution)/shard_map/ppermute | solution.py:368
  118.6 4.3 %collective-permute-start.15 = (f32[4,1,4,8,128]{4,3,2,1,0:T(8,128)S(1)}, f32[4,1,4,8,128]{4,3,2,1,0:T(8,128)S(1)}, u32[]{:S(2)}, u32[]{:S(2)}) collective-permute-start(f32[4,1,4,8,128]{4,3,2,1,0:T(8,128)S(1)} %get-tuple-element.13), channel_id=1, source_target_pairs={{4,0},{8,4},{12,8},{16,12},{20,16},{24,20},{28,24},{0,28},{5,1},{9... | collective-permute-start | bytes 196616 | tf_op jit(solution)/shard_map/ppermute | solution.py:369
  122.9 5.0 %collective-permute-start.16 = (f32[4,6,1,8,128]{4,3,2,1,0:T(8,128)S(1)}, f32[4,6,1,8,128]{4,3,2,1,0:T(8,128)S(1)}, u32[]{:S(2)}, u32[]{:S(2)}) collective-permute-start(f32[4,6,1,8,128]{4,3,2,1,0:T(8,128)S(1)} %get-tuple-element.8), channel_id=1, source_target_pairs={{0,1},{1,2},{2,3},{3,0},{4,5},{5,6},{6,7},{7,4},{8,9},{9,10},{10,1... | collective-permute-start | bytes 294920 | tf_op jit(solution)/shard_map/ppermute | solution.py:368
  125.6 4.6 %collective-permute-start.17 = (f32[4,6,1,8,128]{4,3,2,1,0:T(8,128)S(1)}, f32[4,6,1,8,128]{4,3,2,1,0:T(8,128)S(1)}, u32[]{:S(2)}, u32[]{:S(2)}) collective-permute-start(f32[4,6,1,8,128]{4,3,2,1,0:T(8,128)S(1)} %get-tuple-element.9), channel_id=1, source_target_pairs={{1,0},{2,1},{3,2},{0,3},{5,4},{6,5},{7,6},{4,7},{9,8},{10,9},{11,1... | collective-permute-start | bytes 294920 | tf_op jit(solution)/shard_map/ppermute | solution.py:369
  156.1 3.9 %copy-start = (f32[32,128]{1,0:T(8,128)S(1)}, f32[32,128]{1,0:T(8,128)}, u32[]{:S(2)}) copy-start(f32[32,128]{1,0:T(8,128)} %density.3) | copy-start | bytes 49156
  156.9 3.1 %collective-permute-start.18 = (f32[1,4,4,128]{3,2,1,0:T(4,128)S(1)}, f32[1,4,4,128]{3,2,1,0:T(4,128)S(1)}, u32[]{:S(2)}, u32[]{:S(2)}) collective-permute-start(f32[1,4,4,128]{3,2,1,0:T(4,128)S(1)} %bitcast.44), channel_id=1, source_target_pairs={{0,32},{32,64},{64,96},{96,128},{128,160},{160,192},{192,224},{224... | collective-permute-start | bytes 24584 | tf_op jit(solution)/shard_map/ppermute | solution.py:368
  156.9 3.1 %collective-permute-start.19 = (f32[1,4,4,128]{3,2,1,0:T(4,128)S(1)}, f32[1,4,4,128]{3,2,1,0:T(4,128)S(1)}, u32[]{:S(2)}, u32[]{:S(2)}) collective-permute-start(f32[1,4,4,128]{3,2,1,0:T(4,128)S(1)} %bitcast.42), channel_id=1, source_target_pairs={{32,0},{64,32},{96,64},{128,96},{160,128},{192,160},{224,192},{0,2... | collective-permute-start | bytes 24584 | tf_op jit(solution)/shard_map/ppermute | solution.py:369
  160.0 7.0 %copy-start.4 = (pred[32,32]{1,0:T(32,128)(4,1)S(1)}, pred[32,32]{1,0:T(32,128)(4,1)}, u32[]{:S(2)}) copy-start(pred[32,32]{1,0:T(32,128)(4,1)} %constant.33.clone) | copy-start | bytes 3076
  160.0 8.3 %collective-permute-start.20 = (f32[4,1,4,128]{3,2,1,0:T(4,128)S(1)}, f32[4,1,4,128]{3,2,1,0:T(4,128)S(1)}, u32[]{:S(2)}, u32[]{:S(2)}) collective-permute-start(f32[4,1,4,128]{3,2,1,0:T(4,128)S(1)} %get-tuple-element.24), channel_id=1, source_target_pairs={{0,4},{4,8},{8,12},{12,16},{16,20},{20,24},{24,28},{28,0},{1,5},{5... | collective-permute-start | bytes 24584 | tf_op jit(solution)/shard_map/ppermute | solution.py:368
  167.0 0.7 copy-start.5
  167.0 3.7 %collective-permute-start.21 = (f32[4,1,4,128]{3,2,1,0:T(4,128)S(1)}, f32[4,1,4,128]{3,2,1,0:T(4,128)S(1)}, u32[]{:S(2)}, u32[]{:S(2)}) collective-permute-start(f32[4,1,4,128]{3,2,1,0:T(4,128)S(1)} %get-tuple-element.25), channel_id=1, source_target_pairs={{4,0},{8,4},{12,8},{16,12},{20,16},{24,20},{28,24},{0,28},{5,1},{9... | collective-permute-start | bytes 24584 | tf_op jit(solution)/shard_map/ppermute | solution.py:369
  170.7 3.8 %collective-permute-start.22 = (f32[4,6,1,128]{3,2,1,0:T(1,128)S(1)}, f32[4,6,1,128]{3,2,1,0:T(1,128)S(1)}, u32[]{:S(2)}, u32[]{:S(2)}) collective-permute-start(f32[4,6,1,128]{3,2,1,0:T(1,128)S(1)} %get-tuple-element.20), channel_id=1, source_target_pairs={{0,1},{1,2},{2,3},{3,0},{4,5},{5,6},{6,7},{7,4},{8,9},{9,10},{10,1... | collective-permute-start | bytes 36872 | tf_op jit(solution)/shard_map/ppermute | solution.py:368
  172.1 3.7 %collective-permute-start.23 = (f32[4,6,1,128]{3,2,1,0:T(1,128)S(1)}, f32[4,6,1,128]{3,2,1,0:T(1,128)S(1)}, u32[]{:S(2)}, u32[]{:S(2)}) collective-permute-start(f32[4,6,1,128]{3,2,1,0:T(1,128)S(1)} %get-tuple-element.21), channel_id=1, source_target_pairs={{1,0},{2,1},{3,2},{0,3},{5,4},{6,5},{7,6},{4,7},{9,8},{10,9},{11,1... | collective-permute-start | bytes 36872 | tf_op jit(solution)/shard_map/ppermute | solution.py:369

commit v3 on v2

--- a/solution.py
+++ b/solution.py
@@ -23,7 +23,7 @@
 DISPLACEMENTS = [(a, b, c) for a in (-1, 0, 1) for b in (-1, 0, 1) for c in (-1, 0, 1)]
 ROWS = 32
 UNROLL_MOST = 4
-CHUNK = 8
+CHUNK = 16
 VMEM_LIMIT = 48 * 1024 * 1024
 
 
@@ -65,29 +65,17 @@
     return lax.shift_right_logical(place + (LANES - 1), 7)
 
 
-def spread_columns(wide_ref, number, block, fields, groups):
-    columns = jnp.transpose(block)
-    half = LANES // 2
-
-    def fill(first):
-        for each in range(fields):
-            wide_ref[number, each, pl.ds(first, half), :] = jnp.broadcast_to(
-                columns[first : first + half, each : each + 1], (half, LANES)
-            )
-
-    fill(0)
-
-    @pl.when(groups > half // 8)
-    def _():
-        fill(half)
+def spread_columns(wide_ref, number, block, fields):
+    for each in range(fields):
+        wide_ref[number, each] = jnp.transpose(jnp.broadcast_to(block[each : each + 1], (LANES, LANES)))
 
 
 def own_spot(number, own, grid):
     own_y, own_z = own[1], own[2]
     _, padded_y, padded_z = grid
     at_x = number // (own_y * own_z)
-    at_y = lax.rem(number // own_z, own_y)
-    at_z = lax.rem(number, own_z)
+    at_y = number // own_z % own_y
+    at_z = number % own_z
     return ((at_x + 1) * padded_y + at_y + 1) * padded_z + at_z + 1
 
 
@@ -127,19 +115,22 @@
     lax.fori_loop(0, bins // 4, turn, 0)
 
 
-def density_kernel(own, grid, counts_ref, bins_ref, out_ref, packed_ref, wide_ref, sums_ref, rows_ref):
+def density_kernel(
+    own, grid, counts_ref, bins_ref, out_ref, packed_ref, wide_ref, sums_ref, rows_ref
+):
     bins = own[0] * own[1] * own[2]
     lane = lax.broadcasted_iota(jnp.int32, (8, LANES), 1)
 
-    def groups_of(spot):
-        return jnp.minimum(lax.shift_right_logical(counts_ref[spot] + 8, 3), LANES // 8)
+    def groups_of(number):
+        mine = counts_ref[own_spot(number, own, grid)]
+        return jnp.minimum(lax.shift_right_logical(mine + 8, 3), LANES // 8)
 
     def prepare(number):
         spot = own_spot(number, own, grid)
         rows_ref[number] = pack_sources(
             counts_ref, packed_ref, number, spot, grid, lambda near: bins_ref[near]
         )
-        spread_columns(wide_ref, number, bins_ref[spot], 3, groups_of(spot))
+        spread_columns(wide_ref, number, bins_ref[spot], 3)
 
     each_bin(bins, prepare)
 
@@ -177,7 +168,7 @@
             for g in range(size):
                 sums_ref[number, pl.ds(g * 8, 8), :] = totals[g]
 
-        by_size(groups_of(own_spot(number, own, grid)), 1, LANES // 8, sweep)
+        by_size(groups_of(number), 1, LANES // 8, sweep)
         return carry
 
     lax.fori_loop(0, bins, one_bin, 0)
@@ -204,6 +195,7 @@
     term_ref,
     wide_ref,
     sums_ref,
+    whole_ref,
     rows_ref,
 ):
     bins = own[0] * own[1] * own[2]
@@ -218,28 +210,36 @@
 
         lax.fori_loop(0, slots // 8, clear, 0)
 
-    def groups_of(spot):
-        return lax.shift_right_logical(counts_ref[spot] + 7, 3)
-
-    def whole(near):
-        return jnp.where(field == 7, jnp.broadcast_to(rho_ref[pl.ds(near, 1), :], (8, LANES)), bins_ref[near])
+    def groups_of(number):
+        return lax.shift_right_logical(counts_ref[own_spot(number, own, grid)] + 7, 3)
+
+    def fill(turn, carry):
+        for part in range(8):
+            near = turn * 8 + part
+            rho = jnp.broadcast_to(rho_ref[pl.ds(near, 1), :], (8, LANES))
+            whole_ref[near] = jnp.where(field == 7, rho, bins_ref[near])
+        return carry
+
+    lax.fori_loop(0, whole_ref.shape[0] // 8, fill, 0)
 
     def prepare(number):
         spot = own_spot(number, own, grid)
-        rows_ref[number] = pack_sources(counts_ref, packed_ref, number, spot, grid, whole)
+        rows_ref[number] = pack_sources(
+            counts_ref, packed_ref, number, spot, grid, lambda near: whole_ref[near]
+        )
+        block = whole_ref[spot]
+        rho = jnp.maximum(block, FLOOR)
+        mixed = jnp.where(field == 6, pressure_term(pltpu.roll(rho, 7, 0)), block)
+        spread_columns(wide_ref, number, jnp.where(field == 7, rho * (1.0 / VISCOSITY), mixed), 8)
         density = jnp.maximum(packed_ref[number, :, 7, :], FLOOR)
         term_ref[number, 0] = pressure_term(density)
         term_ref[number, 1] = density * (1.0 / VISCOSITY)
-        my_rho = jnp.broadcast_to(jnp.maximum(rho_ref[pl.ds(spot, 1), :], FLOOR), (8, LANES))
-        mixed = jnp.where(field == 6, pressure_term(my_rho), bins_ref[spot])
-        mixed = jnp.where(field == 7, my_rho * (1.0 / VISCOSITY), mixed)
-        spread_columns(wide_ref, number, mixed, 8, groups_of(spot))
 
     each_bin(bins, prepare)
 
     def one_bin(number, carry):
         rows = rows_ref[number]
-        groups = groups_of(own_spot(number, own, grid))
+        groups = groups_of(number)
 
         def chunk(index, carry):
             half = jnp.where(groups > CHUNK, lax.shift_right_logical(groups + 1, 1), groups)
@@ -351,6 +351,7 @@
             pltpu.VMEM((number, 2, ROWS, LANES), jnp.float32),
             pltpu.VMEM((number, 8, LANES, LANES), jnp.float32),
             pltpu.VMEM((number, 3, LANES, LANES), jnp.float32),
+            pltpu.VMEM(bins.shape, jnp.float32),
             pltpu.SMEM((number,), jnp.int32),
         ],
         compiler_params=pltpu.CompilerParams(vmem_limit_bytes=VMEM_LIMIT),

time: 254 us -> 239 us (0.941); the launches traced: 249 us -> 240 us
  Pallas kernels: 136 us -> 131 us
  starting transfers between devices: 43.9 us -> 38.9 us
    ppermute x12, starting transfers between devices: 29.6 us -> 21.1 us  [extended(): before = lax.ppermute(last, axis, up)]
    pallas_call x2, Pallas kernels: 51 us -> 46.5 us  [density_of(): pl.pallas_call(functools.partial(density_kernel, own, grid), out_shape=ja...]
    ppermute x12, waiting for transfers between devices: 12.1 us -> 8.39 us  [extended(): after = lax.ppermute(initial, axis, down)]
    ppermute x12, starting transfers between devices: 14.3 us -> 17.8 us  [extended(): after = lax.ppermute(initial, axis, down)]
where the time goes in v3:
time: 239 us; the launch traced here: 240 us
  Pallas kernels  131 us (55%)
  starting transfers between devices  38.9 us (16%)
  blocking collectives  32.3 us (14%)
  waiting for transfers between devices  31.2 us (13%)
  local copies, waits for them, and re-layouts  2.88 us (1%)
    pallas_call x2, Pallas kernels, moved(): pl.pallas_call(functools.partial(accel_kernel, own, grid), out_shape=jax....  84.8 us
    pallas_call x2, Pallas kernels, density_of(): pl.pallas_call(functools.partial(density_kernel, own, grid), out_shape=ja...  46.5 us
    all_to_all x1, blocking collectives, local(): lax.all_to_all(states, ('gx', 'gy'), split_axis=0, concat_axis=0, tiled=T...  32.3 us
    ppermute x12, waiting for transfers between devices, extended(): before = lax.ppermute(last, axis, up)  22.8 us
    ppermute x12, starting transfers between devices, extended(): before = lax.ppermute(last, axis, up)  21.1 us
    ppermute x12, starting transfers between devices, extended(): after = lax.ppermute(initial, axis, down)  17.8 us
    ppermute x12, waiting for transfers between devices, extended(): after = lax.ppermute(initial, axis, down)  8.39 us
  transfers between devices with their start and end apart: 24, of which 19 were waited for; matrix products, arithmetic and copies ran while one was open for 0% of the time, Pallas kernels for 0%

profile of v3, /device:TPU:10, one launch (start us, length us, event | category | flops | bytes accessed | tf_op | source)
XLA Modules:
  0.0 239.7 jit_solution(11368694830780377827)
XLA Ops:
  1.8 1.7 collective-permute-start.1
  3.5 1.9 collective-permute-done
  5.5 2.0 collective-permute-start.2
  7.5 4.0 %collective-permute-start.3 = (f32[4,1,4,8,128]{4,2,1,0,3:T(4,128)S(1)}, f32[4,1,4,8,128]{4,2,1,0,3:T(4,128)S(1)}, u32[]{:S(2)}, u32[]{:S(2)}) collective-permute-start(f32[4,1,4,8,128]{4,2,1,0,3:T(4,128)S(1)} %get-tuple-element.15), channel_id=1, source_target_pairs={{4,0},{8,4},{12,8},{16,12},{20,16},{24,20},{28,24},{0,28},{5,1},{9... | collective-permute-start | bytes 196616 | tf_op jit(solution)/shard_map/ppermute | solution.py:370
  11.6 2.1 collective-permute-done.2
  13.9 1.6 collective-permute-start.4
  16.2 3.3 %collective-permute-done.4 = f32[4,6,1,8,128]{4,2,1,0,3:T(1,128)S(1)} collective-permute-done((f32[4,6,1,8,128]{4,2,1,0,3:T(1,128)S(1)}, f32[4,6,1,8,128]{4,2,1,0,3:T(1,128)S(1)}, u32[]{:S(2)}, u32[]{:S(2)}) %collective-permute-start.4) | collective-permute-done | bytes 98336 | tf_op jit(solution)/shard_map/ppermute | solution.py:369
  21.6 23.0 %density.2 = f32[32,128]{1,0:T(8,128)S(1)} custom-call(s32[144]{0:T(256)S(1)} %convert_reduce_fusion.counts_ref, f32[144,8,128]{2,1,0:T(8,128)S(1)} %bitcast.23), custom_call_target="tpu_custom_call" | custom-call | tf_op jit(solution)/shard_map/density/pallas_call | solution.py:326
  44.6 1.7 collective-permute-start.7
  46.3 1.3 collective-permute-done.6
  47.7 3.0 %collective-permute-start.8 = (f32[4,1,4,128]{3,2,1,0:T(4,128)S(1)}, f32[4,1,4,128]{3,2,1,0:T(4,128)S(1)}, u32[]{:S(2)}, u32[]{:S(2)}) collective-permute-start(f32[4,1,4,128]{3,2,1,0:T(4,128)S(1)} %get-tuple-element.26), channel_id=1, source_target_pairs={{0,4},{4,8},{8,12},{12,16},{16,20},{20,24},{24,28},{28,0},{1,5},{5... | collective-permute-start | bytes 24584 | tf_op jit(solution)/shard_map/ppermute | solution.py:369
  51.0 1.6 collective-permute-done.8
  52.6 1.8 collective-permute-done.9
  54.5 2.0 collective-permute-start.11
  56.5 1.8 collective-permute-done.10
  58.6 42.4 %accel.2 = f32[32,8,128]{2,1,0:T(8,128)S(1)} custom-call(s32[144]{0:T(256)S(1)} %convert_reduce_fusion.counts_ref, s32[32]{0:T(128)S(1)} %iota.39.where_ref, f32[144,8,128]{2,1,0:T(8,128)S(1)} %bitcast.24, f32[144,128]{1,0:T(8,128)S(1)} %reshape.102.rho_ref), custom_call_target="tpu_custom_call" | custom-call | tf_op jit(solution)/shard_map/accel/pallas_call | solution.py:344
  101.0 1.7 collective-permute-start.13
  102.8 1.9 collective-permute-done.12
  104.7 10.1 %collective-permute-start.14 = (f32[4,1,4,8,128]{4,3,2,1,0:T(8,128)S(1)}, f32[4,1,4,8,128]{4,3,2,1,0:T(8,128)S(1)}, u32[]{:S(2)}, u32[]{:S(2)}) collective-permute-start(f32[4,1,4,8,128]{4,3,2,1,0:T(8,128)S(1)} %get-tuple-element.12), channel_id=1, source_target_pairs={{0,4},{4,8},{8,12},{12,16},{16,20},{20,24},{24,28},{28,0},{1,5},{5... | collective-permute-start | bytes 196616 | tf_op jit(solution)/shard_map/ppermute | solution.py:369
  114.8 1.9 collective-permute-done.14
  116.7 2.4 collective-permute-done.15
  119.2 2.0 collective-permute-start.17
  121.2 3.2 %collective-permute-done.16 = f32[4,6,1,8,128]{4,3,2,1,0:T(8,128)S(1)} collective-permute-done((f32[4,6,1,8,128]{4,3,2,1,0:T(8,128)S(1)}, f32[4,6,1,8,128]{4,3,2,1,0:T(8,128)S(1)}, u32[]{:S(2)}, u32[]{:S(2)}) %collective-permute-start.16) | collective-permute-done | bytes 98336 | tf_op jit(solution)/shard_map/ppermute | solution.py:369
  124.5 23.6 %density.3 = f32[32,128]{1,0:T(8,128)} custom-call(s32[144]{0:T(256)S(1)} %convert_reduce_fusion.counts_ref, f32[144,8,128]{2,1,0:T(8,128)S(1)} %bitcast.25), custom_call_target="tpu_custom_call" | custom-call | tf_op jit(solution)/shard_map/density/pallas_call | solution.py:326
  148.8 1.7 collective-permute-start.19
  150.6 1.3 collective-permute-done.18
  152.0 4.1 %collective-permute-start.20 = (f32[4,1,4,128]{3,2,1,0:T(4,128)S(1)}, f32[4,1,4,128]{3,2,1,0:T(4,128)S(1)}, u32[]{:S(2)}, u32[]{:S(2)}) collective-permute-start(f32[4,1,4,128]{3,2,1,0:T(4,128)S(1)} %get-tuple-element.24), channel_id=1, source_target_pairs={{0,4},{4,8},{8,12},{12,16},{16,20},{20,24},{24,28},{28,0},{1,5},{5... | collective-permute-start | bytes 24584 | tf_op jit(solution)/shard_map/ppermute | solution.py:369
  157.5 2.3 collective-permute-done.21
  159.9 2.0 collective-permute-start.23
  161.9 1.8 collective-permute-done.22
  164.0 42.5 %accel.3 = f32[128,8,128]{2,1,0:T(8,128)S(1)} custom-call(s32[144]{0:T(256)S(1)} %convert_reduce_fusion.counts_ref, s32[32]{0:T(128)S(1)} %multiply_add_fusion.where_ref, f32[144,8,128]{2,1,0:T(8,128)S(1)} %bitcast.26, f32[144,128]{1,0:T(8,128)S(1)} %reshape.106.rho_ref), custom_call_target="tpu_custom_call" | custom-call | tf_op jit(solution)/shard_map/accel/pallas_call | solution.py:344
  206.5 32.3 %all_to_all.5 = f32[128,8,128]{2,1,0:T(8,128)S(1)} all-to-all(f32[128,8,128]{2,1,0:T(8,128)S(1)} %accel.3), channel_id=1, replica_groups=mesh['gx'=8,'gy'=8,'gz'=4] {'gx','gy'}, dimensions={0} | all-to-all | bytes 1048576 | tf_op jit(solution)/shard_map/all_to_all | solution.py:421
  (66 shorter events, 8.7 us)
Async XLA Ops:
  0.6 0.9 copy-start.3
  0.6 1.0 copy-start.1
  0.7 1.0 copy-start.2
  1.8 3.7 %collective-permute-start = (f32[1,4,4,8,128]{4,2,1,0,3:T(4,128)S(1)}, f32[1,4,4,8,128]{4,2,1,0,3:T(4,128)S(1)}, u32[]{:S(2)}, u32[]{:S(2)}) collective-permute-start(f32[1,4,4,8,128]{4,2,1,0,3:T(4,128)S(1)} %get-tuple-element.18), channel_id=1, source_target_pairs={{0,32},{32,64},{64,96},{96,128},{128,160},{160,192},{192,224},{224... | collective-permute-start | bytes 196616 | tf_op jit(solution)/shard_map/ppermute | solution.py:369
  1.8 3.7 %collective-permute-start.1 = (f32[1,4,4,8,128]{4,2,1,0,3:T(4,128)S(1)}, f32[1,4,4,8,128]{4,2,1,0,3:T(4,128)S(1)}, u32[]{:S(2)}, u32[]{:S(2)}) collective-permute-start(f32[1,4,4,8,128]{4,2,1,0,3:T(4,128)S(1)} %get-tuple-element.19), channel_id=1, source_target_pairs={{32,0},{64,32},{96,64},{128,96},{160,128},{192,160},{224,192},{0,2... | collective-permute-start | bytes 196616 | tf_op jit(solution)/shard_map/ppermute | solution.py:370
  5.5 8.2 %collective-permute-start.2 = (f32[4,1,4,8,128]{4,2,1,0,3:T(4,128)S(1)}, f32[4,1,4,8,128]{4,2,1,0,3:T(4,128)S(1)}, u32[]{:S(2)}, u32[]{:S(2)}) collective-permute-start(f32[4,1,4,8,128]{4,2,1,0,3:T(4,128)S(1)} %get-tuple-element.14), channel_id=1, source_target_pairs={{0,4},{4,8},{8,12},{12,16},{16,20},{20,24},{24,28},{28,0},{1,5},{5... | collective-permute-start | bytes 196616 | tf_op jit(solution)/shard_map/ppermute | solution.py:369
  7.5 6.2 %collective-permute-start.3 = (f32[4,1,4,8,128]{4,2,1,0,3:T(4,128)S(1)}, f32[4,1,4,8,128]{4,2,1,0,3:T(4,128)S(1)}, u32[]{:S(2)}, u32[]{:S(2)}) collective-permute-start(f32[4,1,4,8,128]{4,2,1,0,3:T(4,128)S(1)} %get-tuple-element.15), channel_id=1, source_target_pairs={{4,0},{8,4},{12,8},{16,12},{20,16},{24,20},{28,24},{0,28},{5,1},{9... | collective-permute-start | bytes 196616 | tf_op jit(solution)/shard_map/ppermute | solution.py:370
  13.9 5.6 %collective-permute-start.4 = (f32[4,6,1,8,128]{4,2,1,0,3:T(1,128)S(1)}, f32[4,6,1,8,128]{4,2,1,0,3:T(1,128)S(1)}, u32[]{:S(2)}, u32[]{:S(2)}) collective-permute-start(f32[4,6,1,8,128]{4,2,1,0,3:T(1,128)S(1)} %get-tuple-element.10), channel_id=1, source_target_pairs={{0,1},{1,2},{2,3},{3,0},{4,5},{5,6},{6,7},{7,4},{8,9},{9,10},{10,1... | collective-permute-start | bytes 294920 | tf_op jit(solution)/shard_map/ppermute | solution.py:369
  15.4 5.2 %collective-permute-start.5 = (f32[4,6,1,8,128]{4,2,1,0,3:T(1,128)S(1)}, f32[4,6,1,8,128]{4,2,1,0,3:T(1,128)S(1)}, u32[]{:S(2)}, u32[]{:S(2)}) collective-permute-start(f32[4,6,1,8,128]{4,2,1,0,3:T(1,128)S(1)} %get-tuple-element.11), channel_id=1, source_target_pairs={{1,0},{2,1},{3,2},{0,3},{5,4},{6,5},{7,6},{4,7},{9,8},{10,9},{11,1... | collective-permute-start | bytes 294920 | tf_op jit(solution)/shard_map/ppermute | solution.py:370
  44.6 3.1 %collective-permute-start.6 = (f32[1,4,4,128]{3,2,1,0:T(4,128)S(1)}, f32[1,4,4,128]{3,2,1,0:T(4,128)S(1)}, u32[]{:S(2)}, u32[]{:S(2)}) collective-permute-start(f32[1,4,4,128]{3,2,1,0:T(4,128)S(1)} %bitcast.43), channel_id=1, source_target_pairs={{0,32},{32,64},{64,96},{96,128},{128,160},{160,192},{192,224},{224... | collective-permute-start | bytes 24584 | tf_op jit(solution)/shard_map/ppermute | solution.py:369
  44.6 3.1 %collective-permute-start.7 = (f32[1,4,4,128]{3,2,1,0:T(4,128)S(1)}, f32[1,4,4,128]{3,2,1,0:T(4,128)S(1)}, u32[]{:S(2)}, u32[]{:S(2)}) collective-permute-start(f32[1,4,4,128]{3,2,1,0:T(4,128)S(1)} %bitcast.41), channel_id=1, source_target_pairs={{32,0},{64,32},{96,64},{128,96},{160,128},{192,160},{224,192},{0,2... | collective-permute-start | bytes 24584 | tf_op jit(solution)/shard_map/ppermute | solution.py:370
  47.7 4.9 %collective-permute-start.8 = (f32[4,1,4,128]{3,2,1,0:T(4,128)S(1)}, f32[4,1,4,128]{3,2,1,0:T(4,128)S(1)}, u32[]{:S(2)}, u32[]{:S(2)}) collective-permute-start(f32[4,1,4,128]{3,2,1,0:T(4,128)S(1)} %get-tuple-element.26), channel_id=1, source_target_pairs={{0,4},{4,8},{8,12},{12,16},{16,20},{20,24},{24,28},{28,0},{1,5},{5... | collective-permute-start | bytes 24584 | tf_op jit(solution)/shard_map/ppermute | solution.py:369
  50.7 3.7 %collective-permute-start.9 = (f32[4,1,4,128]{3,2,1,0:T(4,128)S(1)}, f32[4,1,4,128]{3,2,1,0:T(4,128)S(1)}, u32[]{:S(2)}, u32[]{:S(2)}) collective-permute-start(f32[4,1,4,128]{3,2,1,0:T(4,128)S(1)} %get-tuple-element.27), channel_id=1, source_target_pairs={{4,0},{8,4},{12,8},{16,12},{20,16},{24,20},{28,24},{0,28},{5,1},{9... | collective-permute-start | bytes 24584 | tf_op jit(solution)/shard_map/ppermute | solution.py:370
  54.4 3.9 %collective-permute-start.10 = (f32[4,6,1,128]{3,2,1,0:T(1,128)S(1)}, f32[4,6,1,128]{3,2,1,0:T(1,128)S(1)}, u32[]{:S(2)}, u32[]{:S(2)}) collective-permute-start(f32[4,6,1,128]{3,2,1,0:T(1,128)S(1)} %get-tuple-element.22), channel_id=1, source_target_pairs={{0,1},{1,2},{2,3},{3,0},{4,5},{5,6},{6,7},{7,4},{8,9},{9,10},{10,1... | collective-permute-start | bytes 36872 | tf_op jit(solution)/shard_map/ppermute | solution.py:369
  54.5 4.1 %collective-permute-start.11 = (f32[4,6,1,128]{3,2,1,0:T(1,128)S(1)}, f32[4,6,1,128]{3,2,1,0:T(1,128)S(1)}, u32[]{:S(2)}, u32[]{:S(2)}) collective-permute-start(f32[4,6,1,128]{3,2,1,0:T(1,128)S(1)} %get-tuple-element.23), channel_id=1, source_target_pairs={{1,0},{2,1},{3,2},{0,3},{5,4},{6,5},{7,6},{4,7},{9,8},{10,9},{11,1... | collective-permute-start | bytes 36872 | tf_op jit(solution)/shard_map/ppermute | solution.py:370
  101.0 3.7 %collective-permute-start.12 = (f32[1,4,4,8,128]{4,3,2,1,0:T(8,128)S(1)}, f32[1,4,4,8,128]{4,3,2,1,0:T(8,128)S(1)}, u32[]{:S(2)}, u32[]{:S(2)}) collective-permute-start(f32[1,4,4,8,128]{4,3,2,1,0:T(8,128)S(1)} %bitcast.39), channel_id=1, source_target_pairs={{0,32},{32,64},{64,96},{96,128},{128,160},{160,192},{192,224},{224... | collective-permute-start | bytes 196616 | tf_op jit(solution)/shard_map/ppermute | solution.py:369
  101.0 3.7 %collective-permute-start.13 = (f32[1,4,4,8,128]{4,3,2,1,0:T(8,128)S(1)}, f32[1,4,4,8,128]{4,3,2,1,0:T(8,128)S(1)}, u32[]{:S(2)}, u32[]{:S(2)}) collective-permute-start(f32[1,4,4,8,128]{4,3,2,1,0:T(8,128)S(1)} %bitcast.38), channel_id=1, source_target_pairs={{32,0},{64,32},{96,64},{128,96},{160,128},{192,160},{224,192},{0,2... | collective-permute-start | bytes 196616 | tf_op jit(solution)/shard_map/ppermute | solution.py:370
  104.7 12.0 %collective-permute-start.14 = (f32[4,1,4,8,128]{4,3,2,1,0:T(8,128)S(1)}, f32[4,1,4,8,128]{4,3,2,1,0:T(8,128)S(1)}, u32[]{:S(2)}, u32[]{:S(2)}) collective-permute-start(f32[4,1,4,8,128]{4,3,2,1,0:T(8,128)S(1)} %get-tuple-element.12), channel_id=1, source_target_pairs={{0,4},{4,8},{8,12},{12,16},{16,20},{20,24},{24,28},{28,0},{1,5},{5... | collective-permute-start | bytes 196616 | tf_op jit(solution)/shard_map/ppermute | solution.py:369
  114.8 4.3 %collective-permute-start.15 = (f32[4,1,4,8,128]{4,3,2,1,0:T(8,128)S(1)}, f32[4,1,4,8,128]{4,3,2,1,0:T(8,128)S(1)}, u32[]{:S(2)}, u32[]{:S(2)}) collective-permute-start(f32[4,1,4,8,128]{4,3,2,1,0:T(8,128)S(1)} %get-tuple-element.13), channel_id=1, source_target_pairs={{4,0},{8,4},{12,8},{16,12},{20,16},{24,20},{28,24},{0,28},{5,1},{9... | collective-permute-start | bytes 196616 | tf_op jit(solution)/shard_map/ppermute | solution.py:370
  119.1 5.3 %collective-permute-start.16 = (f32[4,6,1,8,128]{4,3,2,1,0:T(8,128)S(1)}, f32[4,6,1,8,128]{4,3,2,1,0:T(8,128)S(1)}, u32[]{:S(2)}, u32[]{:S(2)}) collective-permute-start(f32[4,6,1,8,128]{4,3,2,1,0:T(8,128)S(1)} %get-tuple-element.8), channel_id=1, source_target_pairs={{0,1},{1,2},{2,3},{3,0},{4,5},{5,6},{6,7},{7,4},{8,9},{9,10},{10,1... | collective-permute-start | bytes 294920 | tf_op jit(solution)/shard_map/ppermute | solution.py:369
  119.2 5.3 %collective-permute-start.17 = (f32[4,6,1,8,128]{4,3,2,1,0:T(8,128)S(1)}, f32[4,6,1,8,128]{4,3,2,1,0:T(8,128)S(1)}, u32[]{:S(2)}, u32[]{:S(2)}) collective-permute-start(f32[4,6,1,8,128]{4,3,2,1,0:T(8,128)S(1)} %get-tuple-element.9), channel_id=1, source_target_pairs={{1,0},{2,1},{3,2},{0,3},{5,4},{6,5},{7,6},{4,7},{9,8},{10,9},{11,1... | collective-permute-start | bytes 294920 | tf_op jit(solution)/shard_map/ppermute | solution.py:370
  148.0 3.9 %copy-start = (f32[32,128]{1,0:T(8,128)S(1)}, f32[32,128]{1,0:T(8,128)}, u32[]{:S(2)}) copy-start(f32[32,128]{1,0:T(8,128)} %density.3) | copy-start | bytes 49156
  148.8 3.1 %collective-permute-start.18 = (f32[1,4,4,128]{3,2,1,0:T(4,128)S(1)}, f32[1,4,4,128]{3,2,1,0:T(4,128)S(1)}, u32[]{:S(2)}, u32[]{:S(2)}) collective-permute-start(f32[1,4,4,128]{3,2,1,0:T(4,128)S(1)} %bitcast.44), channel_id=1, source_target_pairs={{0,32},{32,64},{64,96},{96,128},{128,160},{160,192},{192,224},{224... | collective-permute-start | bytes 24584 | tf_op jit(solution)/shard_map/ppermute | solution.py:369
  148.8 3.1 %collective-permute-start.19 = (f32[1,4,4,128]{3,2,1,0:T(4,128)S(1)}, f32[1,4,4,128]{3,2,1,0:T(4,128)S(1)}, u32[]{:S(2)}, u32[]{:S(2)}) collective-permute-start(f32[1,4,4,128]{3,2,1,0:T(4,128)S(1)} %bitcast.42), channel_id=1, source_target_pairs={{32,0},{64,32},{96,64},{128,96},{160,128},{192,160},{224,192},{0,2... | collective-permute-start | bytes 24584 | tf_op jit(solution)/shard_map/ppermute | solution.py:370
  151.9 4.2 %copy-start.4 = (pred[32,32]{1,0:T(32,128)(4,1)S(1)}, pred[32,32]{1,0:T(32,128)(4,1)}, u32[]{:S(2)}) copy-start(pred[32,32]{1,0:T(32,128)(4,1)} %constant.33.clone) | copy-start | bytes 3076
  152.0 5.5 %collective-permute-start.20 = (f32[4,1,4,128]{3,2,1,0:T(4,128)S(1)}, f32[4,1,4,128]{3,2,1,0:T(4,128)S(1)}, u32[]{:S(2)}, u32[]{:S(2)}) collective-permute-start(f32[4,1,4,128]{3,2,1,0:T(4,128)S(1)} %get-tuple-element.24), channel_id=1, source_target_pairs={{0,4},{4,8},{8,12},{12,16},{16,20},{20,24},{24,28},{28,0},{1,5},{5... | collective-permute-start | bytes 24584 | tf_op jit(solution)/shard_map/ppermute | solution.py:369
  156.1 0.7 copy-start.5
  156.1 3.7 %collective-permute-start.21 = (f32[4,1,4,128]{3,2,1,0:T(4,128)S(1)}, f32[4,1,4,128]{3,2,1,0:T(4,128)S(1)}, u32[]{:S(2)}, u32[]{:S(2)}) collective-permute-start(f32[4,1,4,128]{3,2,1,0:T(4,128)S(1)} %get-tuple-element.25), channel_id=1, source_target_pairs={{4,0},{8,4},{12,8},{16,12},{20,16},{24,20},{28,24},{0,28},{5,1},{9... | collective-permute-start | bytes 24584 | tf_op jit(solution)/shard_map/ppermute | solution.py:370
  159.8 3.9 %collective-permute-start.22 = (f32[4,6,1,128]{3,2,1,0:T(1,128)S(1)}, f32[4,6,1,128]{3,2,1,0:T(1,128)S(1)}, u32[]{:S(2)}, u32[]{:S(2)}) collective-permute-start(f32[4,6,1,128]{3,2,1,0:T(1,128)S(1)} %get-tuple-element.20), channel_id=1, source_target_pairs={{0,1},{1,2},{2,3},{3,0},{4,5},{5,6},{6,7},{7,4},{8,9},{9,10},{10,1... | collective-permute-start | bytes 36872 | tf_op jit(solution)/shard_map/ppermute | solution.py:369
  159.9 4.1 %collective-permute-start.23 = (f32[4,6,1,128]{3,2,1,0:T(1,128)S(1)}, f32[4,6,1,128]{3,2,1,0:T(1,128)S(1)}, u32[]{:S(2)}, u32[]{:S(2)}) collective-permute-start(f32[4,6,1,128]{3,2,1,0:T(1,128)S(1)} %get-tuple-element.21), channel_id=1, source_target_pairs={{1,0},{2,1},{3,2},{0,3},{5,4},{6,5},{7,6},{4,7},{9,8},{10,9},{11,1... | collective-permute-start | bytes 36872 | tf_op jit(solution)/shard_map/ppermute | solution.py:370

commit v4 on v3

--- a/solution.py
+++ b/solution.py
@@ -24,7 +24,7 @@
 ROWS = 32
 UNROLL_MOST = 4
 CHUNK = 16
-VMEM_LIMIT = 48 * 1024 * 1024
+VMEM_LIMIT = 34 * 1024 * 1024
 
 
 def pressure_term(density):
@@ -116,7 +116,7 @@
 
 
 def density_kernel(
-    own, grid, counts_ref, bins_ref, out_ref, packed_ref, wide_ref, sums_ref, rows_ref
+    own, grid, counts_ref, bins_ref, wide_ref, out_ref, packed_ref, sums_ref, rows_ref
 ):
     bins = own[0] * own[1] * own[2]
     lane = lax.broadcasted_iota(jnp.int32, (8, LANES), 1)
@@ -130,7 +130,6 @@
         rows_ref[number] = pack_sources(
             counts_ref, packed_ref, number, spot, grid, lambda near: bins_ref[near]
         )
-        spread_columns(wide_ref, number, bins_ref[spot], 3)
 
     each_bin(bins, prepare)
 
@@ -190,10 +189,12 @@
     where_ref,
     bins_ref,
     rho_ref,
+    wide_ref,
+    speed_ref,
     out_ref,
     packed_ref,
     term_ref,
-    wide_ref,
+    own_term_ref,
     sums_ref,
     whole_ref,
     rows_ref,
@@ -229,8 +230,8 @@
         )
         block = whole_ref[spot]
         rho = jnp.maximum(block, FLOOR)
-        mixed = jnp.where(field == 6, pressure_term(pltpu.roll(rho, 7, 0)), block)
-        spread_columns(wide_ref, number, jnp.where(field == 7, rho * (1.0 / VISCOSITY), mixed), 8)
+        terms = jnp.where(field == 7, rho * (1.0 / VISCOSITY), pressure_term(pltpu.roll(rho, 7, 0)))
+        spread_columns(own_term_ref, number, terms[6:8], 2)
         density = jnp.maximum(packed_ref[number, :, 7, :], FLOOR)
         term_ref[number, 0] = pressure_term(density)
         term_ref[number, 1] = density * (1.0 / VISCOSITY)
@@ -263,17 +264,17 @@
                             z = wide_ref[number, 2, at[g], :] - near[2]
                             square = x * x + y * y + z * z
                             approach = (
-                                (wide_ref[number, 3, at[g], :] - near[3]) * x
-                                + (wide_ref[number, 4, at[g], :] - near[4]) * y
-                                + (wide_ref[number, 5, at[g], :] - near[5]) * z
+                                (speed_ref[number, 0, at[g], :] - near[3]) * x
+                                + (speed_ref[number, 1, at[g], :] - near[4]) * y
+                                + (speed_ref[number, 2, at[g], :] - near[5]) * z
                             )
                             approach = jnp.minimum(approach, 0.0)
-                            below = (square + 0.0025) * (wide_ref[number, 7, at[g], :] + near_rho)
+                            below = (square + 0.0025) * (own_term_ref[number, 1, at[g], :] + near_rho)
                             viscous = approach / below
                             square = jnp.maximum(square, TINY)
                             falloff = jnp.maximum(1.0 - square * lax.rsqrt(square), 0.0)
                             third = falloff * falloff * falloff
-                            weight = ((wide_ref[number, 6, at[g], :] + near_term) - viscous) * (near[6] * third)
+                            weight = ((own_term_ref[number, 0, at[g], :] + near_term) - viscous) * (near[6] * third)
                             totals[3 * g] = totals[3 * g] + weight * x
                             totals[3 * g + 1] = totals[3 * g + 1] + weight * y
                             totals[3 * g + 2] = totals[3 * g + 2] + weight * z
@@ -317,46 +318,63 @@
     each_bin(bins, finish)
 
 
+def columns_kernel(first, states_ref, out_ref):
+    for number in range(out_ref.shape[0]):
+        spread_columns(out_ref, number, states_ref[number, first : first + 3], 3)
+
+
 VMEM_SPEC = pl.BlockSpec(memory_space=pltpu.VMEM)
 SMEM_SPEC = pl.BlockSpec(memory_space=pltpu.SMEM)
 
 
-def density_of(counts, bins, own, grid):
+def columns_of(states, bins, first):
+    block = 8
+    return pl.pallas_call(
+        functools.partial(columns_kernel, first),
+        grid=(bins // block,),
+        out_shape=jax.ShapeDtypeStruct((bins, 3, LANES, LANES), jnp.float32),
+        in_specs=[pl.BlockSpec((block, 8, LANES), lambda turn: (turn, 0, 0))],
+        out_specs=pl.BlockSpec((block, 3, LANES, LANES), lambda turn: (turn, 0, 0, 0)),
+        cost_estimate=pl.CostEstimate(flops=0, bytes_accessed=bins * 3 * LANES * LANES * 4, transcendentals=0),
+        name="columns",
+    )(states)
+
+
+def density_of(counts, bins, columns, own, grid):
     number = own[0] * own[1] * own[2]
     return pl.pallas_call(
         functools.partial(density_kernel, own, grid),
         out_shape=jax.ShapeDtypeStruct((number, LANES), jnp.float32),
-        in_specs=[SMEM_SPEC, VMEM_SPEC],
+        in_specs=[SMEM_SPEC, VMEM_SPEC, VMEM_SPEC],
         out_specs=VMEM_SPEC,
         scratch_shapes=[
             pltpu.VMEM((number, ROWS, 8, LANES), jnp.float32),
-            pltpu.VMEM((number, 3, LANES, LANES), jnp.float32),
             pltpu.VMEM((number, LANES, LANES), jnp.float32),
             pltpu.SMEM((number,), jnp.int32),
         ],
         compiler_params=pltpu.CompilerParams(vmem_limit_bytes=VMEM_LIMIT),
         name="density",
-    )(counts, bins)
-
-
-def moved(counts, where_to, bins, rho, own, grid, slots):
+    )(counts, bins, columns)
+
+
+def moved(counts, where_to, bins, rho, places, speeds, own, grid, slots):
     number = own[0] * own[1] * own[2]
     return pl.pallas_call(
         functools.partial(accel_kernel, own, grid),
         out_shape=jax.ShapeDtypeStruct((slots, 8, LANES), jnp.float32),
-        in_specs=[SMEM_SPEC, SMEM_SPEC, VMEM_SPEC, VMEM_SPEC],
+        in_specs=[SMEM_SPEC, SMEM_SPEC, VMEM_SPEC, VMEM_SPEC, VMEM_SPEC, VMEM_SPEC],
         out_specs=VMEM_SPEC,
         scratch_shapes=[
             pltpu.VMEM((number, ROWS, 8, LANES), jnp.float32),
             pltpu.VMEM((number, 2, ROWS, LANES), jnp.float32),
-            pltpu.VMEM((number, 8, LANES, LANES), jnp.float32),
+            pltpu.VMEM((number, 2, LANES, LANES), jnp.float32),
             pltpu.VMEM((number, 3, LANES, LANES), jnp.float32),
             pltpu.VMEM(bins.shape, jnp.float32),
             pltpu.SMEM((number,), jnp.int32),
         ],
         compiler_params=pltpu.CompilerParams(vmem_limit_bytes=VMEM_LIMIT),
         name="accel",
-    )(counts, where_to, bins, rho)
+    )(counts, where_to, bins, rho, places, speeds)
 
 
 def extended(value):
@@ -400,11 +418,15 @@
     in_order = jnp.arange(bins, dtype=jnp.int32)
     near_counts = None
     for substep in range(SUBSTEPS):
+        blocks = states.reshape(bins, 8, LANES)
+        places = columns_of(blocks, bins, 0)
         near = extended(states).reshape(padded, 8, LANES)
         if near_counts is None:
             occupied = (near[:, 6, :] > 0.0) & inside(grid).reshape(padded, 1)
             near_counts = jnp.sum(occupied.astype(jnp.int32), axis=1)
-        density = density_of(near_counts, near, own, grid)
+        density = density_of(near_counts, near, places, own, grid)
+        blocks, density = lax.optimization_barrier((blocks, density))
+        speeds = columns_of(blocks, bins, 3)
         near_rho = extended(density.reshape(own + (LANES,))).reshape(padded, LANES)
         last = substep == SUBSTEPS - 1
         states = moved(
@@ -412,6 +434,8 @@
             where_to if last else in_order,
             near,
             near_rho,
+            places,
+            speeds,
             own,
             grid,
             layers * capacity if last else bins,

time: 239 us -> 262 us (1.096)
  local copies, waits for them, and re-layouts: 2.88 us -> 19.6 us
  blocking collectives: 32.3 us -> 43.2 us
  waiting for transfers between devices: 31.2 us -> 21.9 us
  Pallas kernels: 131 us -> 127 us
  other arithmetic: 2.21 us -> 6.1 us
    pallas_call x0 -> x4, Pallas kernels: none -> 19.4 us  [columns_of(): pl.pallas_call(functools.partial(columns_kernel, first), grid=(bins // bl...]
    pallas_call x2, Pallas kernels: 84.8 us -> 68.4 us  [moved(): pl.pallas_call(functools.partial(accel_kernel, own, grid), out_shape=jax....]
    unnamed x13 -> x21, local copies, waits for them, and re-layouts: 1.52 us -> 17.6 us
    all_to_all x1, blocking collectives: 32.3 us -> 43.2 us  [local(): lax.all_to_all(states, ('gx', 'gy'), split_axis=0, concat_axis=0, tiled=T...]
    ppermute x12, starting transfers between devices: 17.8 us -> 28.6 us  [extended(): after = lax.ppermute(initial, axis, down)]
    ppermute x12, starting transfers between devices: 21.1 us -> 12.6 us  [extended(): before = lax.ppermute(last, axis, up)]
    ppermute x12, waiting for transfers between devices: 22.8 us -> 14.4 us  [extended(): before = lax.ppermute(last, axis, up)]
    pallas_call x2, Pallas kernels: 46.5 us -> 39.6 us  [density_of(): pl.pallas_call(functools.partial(density_kernel, own, grid), out_shape=ja...]
  transfers between devices with their start and end apart: 24 -> 24, of which waited for: 19 -> 14; matrix products, arithmetic and copies ran while one was open for 0% -> 0% of each run, Pallas kernels for 0% -> 7%
where the time goes in v4:
time: 262 us; the launch traced here: 260 us
  Pallas kernels  127 us (48%)
  blocking collectives  43.2 us (16%)
  starting transfers between devices  41.2 us (16%)
  waiting for transfers between devices  21.9 us (8%)
  local copies, waits for them, and re-layouts  19.6 us (7%)
  other arithmetic  6.1 us (2%)
    pallas_call x2, Pallas kernels, moved(): pl.pallas_call(functools.partial(accel_kernel, own, grid), out_shape=jax....  68.4 us
    all_to_all x1, blocking collectives, local(): lax.all_to_all(states, ('gx', 'gy'), split_axis=0, concat_axis=0, tiled=T...  43.2 us
    pallas_call x2, Pallas kernels, density_of(): pl.pallas_call(functools.partial(density_kernel, own, grid), out_shape=ja...  39.6 us
    ppermute x12, starting transfers between devices, extended(): after = lax.ppermute(initial, axis, down)  28.6 us
    pallas_call x4, Pallas kernels, columns_of(): pl.pallas_call(functools.partial(columns_kernel, first), grid=(bins // bl...  19.4 us
    unnamed x21, local copies, waits for them, and re-layouts  17.6 us
    ppermute x12, waiting for transfers between devices, extended(): before = lax.ppermute(last, axis, up)  14.4 us
    ppermute x12, starting transfers between devices, extended(): before = lax.ppermute(last, axis, up)  12.6 us
  transfers between devices with their start and end apart: 24, of which 14 were waited for; matrix products, arithmetic and copies ran while one was open for 0% of the time, Pallas kernels for 7%

profile of v4, /device:TPU:10, one launch (start us, length us, event | category | flops | bytes accessed | tf_op | source)
XLA Modules:
  0.0 260.2 jit_solution(16481149539688572759)
XLA Ops:
  5.0 1.9 collective-permute-done
  7.0 2.0 collective-permute-start.2
  9.0 4.0 %collective-permute-start.3 = (f32[4,1,4,8,128]{4,2,1,0,3:T(4,128)S(1)}, f32[4,1,4,8,128]{4,2,1,0,3:T(4,128)S(1)}, u32[]{:S(2)}, u32[]{:S(2)}) collective-permute-start(f32[4,1,4,8,128]{4,2,1,0,3:T(4,128)S(1)} %get-tuple-element.23), channel_id=1, source_target_pairs={{4,0},{8,4},{12,8},{16,12},{20,16},{24,20},{28,24},{0,28},{5,1},{9... | collective-permute-start | bytes 196616 | tf_op jit(solution)/shard_map/ppermute | solution.py:388
  13.0 2.1 collective-permute-done.2
  18.3 4.9 %columns.4.wide_ref = f32[32,3,128,128]{3,2,1,0:T(8,128)} custom-call(f32[32,8,128]{2,1,0:T(8,128)} %bitcast.35), custom_call_target="tpu_custom_call" | custom-call | bytes 6291456 | tf_op jit(solution)/shard_map/columns/pallas_call | solution.py:332
  24.1 2.8 %copy-done = f32[32,3,128,128]{3,2,1,0:T(8,128)S(1)} copy-done((f32[32,3,128,128]{3,2,1,0:T(8,128)S(1)}, f32[32,3,128,128]{3,2,1,0:T(8,128)}, u32[]{:S(2)}) %copy-start) | copy-done | bytes 6291480
  26.9 19.5 %density.2 = f32[32,128]{1,0:T(8,128)S(1)} custom-call(s32[144]{0:T(256)S(1)} %convert_reduce_fusion.counts_ref, f32[144,8,128]{2,1,0:T(8,128)S(1)} %bitcast.27, f32[32,3,128,128]{3,2,1,0:T(8,128)S(1)} %copy-done), custom_call_target="tpu_custom_call" | custom-call | tf_op jit(solution)/shard_map/density/pallas_call | solution.py:345
  46.4 3.1 %collective-permute-start.7 = (f32[1,4,4,128]{3,2,1,0:T(4,128)S(1)}, f32[1,4,4,128]{3,2,1,0:T(4,128)S(1)}, u32[]{:S(2)}, u32[]{:S(2)}) collective-permute-start(f32[1,4,4,128]{3,2,1,0:T(4,128)S(1)} %bitcast.46), channel_id=1, source_target_pairs={{32,0},{64,32},{96,64},{128,96},{160,128},{192,160},{224,192},{0,2... | collective-permute-start | bytes 24584 | tf_op jit(solution)/shard_map/ppermute | solution.py:388
  52.6 3.2 %collective-permute-start.9 = (f32[4,1,4,128]{3,2,1,0:T(4,128)S(1)}, f32[4,1,4,128]{3,2,1,0:T(4,128)S(1)}, u32[]{:S(2)}, u32[]{:S(2)}) collective-permute-start(f32[4,1,4,128]{3,2,1,0:T(4,128)S(1)} %get-tuple-element.35), channel_id=1, source_target_pairs={{4,0},{8,4},{12,8},{16,12},{20,16},{24,20},{28,24},{0,28},{5,1},{9... | collective-permute-start | bytes 24584 | tf_op jit(solution)/shard_map/ppermute | solution.py:388
  60.2 4.8 %columns.5.speed_ref = f32[32,3,128,128]{3,2,1,0:T(8,128)} custom-call(f32[32,8,128]{2,1,0:T(8,128)} %bitcast.36), custom_call_target="tpu_custom_call" | custom-call | bytes 6291456 | tf_op jit(solution)/shard_map/columns/pallas_call | solution.py:332
  65.1 2.8 %copy-done.1 = f32[32,3,128,128]{3,2,1,0:T(8,128)S(1)} copy-done((f32[32,3,128,128]{3,2,1,0:T(8,128)S(1)}, f32[32,3,128,128]{3,2,1,0:T(8,128)}, u32[]{:S(2)}) %copy-start.1) | copy-done | bytes 6291480
  67.9 2.8 %copy-done.4 = f32[32,3,128,128]{3,2,1,0:T(8,128)S(1)} copy-done((f32[32,3,128,128]{3,2,1,0:T(8,128)S(1)}, f32[32,3,128,128]{3,2,1,0:T(8,128)}, u32[]{:S(2)}) %copy-start.4) | copy-done | bytes 6291480
  70.7 34.2 %accel.2.states_ref = f32[32,8,128]{2,1,0:T(8,128)S(1)} custom-call(s32[144]{0:T(256)S(1)} %convert_reduce_fusion.counts_ref, s32[32]{0:T(128)S(1)} %iota.39.where_ref, f32[144,8,128]{2,1,0:T(8,128)S(1)} %bitcast.28, f32[144,128]{1,0:T(8,128)S(1)} %reshape.106.rho_ref, f32[32,3,128,128]{3,2,1,0:T(8,128)S(1)} %copy-done.1, f32[32,3,128,128]{3,2,1,0:T(8,128)S(1)} %copy-done.4), custom_call_target="tpu_custom_call" | custom-call | tf_op jit(solution)/shard_map/accel/pallas_call | solution.py:362
  104.9 3.3 %collective-permute-start.13 = (f32[1,4,4,8,128]{4,3,2,1,0:T(8,128)S(1)}, f32[1,4,4,8,128]{4,3,2,1,0:T(8,128)S(1)}, u32[]{:S(2)}, u32[]{:S(2)}) collective-permute-start(f32[1,4,4,8,128]{4,3,2,1,0:T(8,128)S(1)} %bitcast.42), channel_id=1, source_target_pairs={{32,0},{64,32},{96,64},{128,96},{160,128},{192,160},{224,192},{0,2... | collective-permute-start | bytes 196616 | tf_op jit(solution)/shard_map/ppermute | solution.py:388
  108.3 1.9 collective-permute-done.13
  110.2 1.8 collective-permute-done.12
  112.0 2.8 %collective-permute-start.14 = (f32[4,1,4,8,128]{4,3,2,1,0:T(8,128)S(1)}, f32[4,1,4,8,128]{4,3,2,1,0:T(8,128)S(1)}, u32[]{:S(2)}, u32[]{:S(2)}) collective-permute-start(f32[4,1,4,8,128]{4,3,2,1,0:T(8,128)S(1)} %get-tuple-element.20), channel_id=1, source_target_pairs={{0,4},{4,8},{8,12},{12,16},{16,20},{20,24},{24,28},{28,0},{1,5},{5... | collective-permute-start | bytes 196616 | tf_op jit(solution)/shard_map/ppermute | solution.py:387
  114.8 1.8 collective-permute-start.15
  116.6 2.2 collective-permute-done.14
  119.1 2.9 %collective-permute-start.16 = (f32[4,6,1,8,128]{4,3,2,1,0:T(8,128)S(1)}, f32[4,6,1,8,128]{4,3,2,1,0:T(8,128)S(1)}, u32[]{:S(2)}, u32[]{:S(2)}) collective-permute-start(f32[4,6,1,8,128]{4,3,2,1,0:T(8,128)S(1)} %get-tuple-element.16), channel_id=1, source_target_pairs={{0,1},{1,2},{2,3},{3,0},{4,5},{5,6},{6,7},{7,4},{8,9},{9,10},{10,1... | collective-permute-start | bytes 294920 | tf_op jit(solution)/shard_map/ppermute | solution.py:387
  122.0 1.9 collective-permute-start.17
  123.9 4.8 %columns.6.wide_ref = f32[32,3,128,128]{3,2,1,0:T(8,128)} custom-call(f32[32,8,128]{2,1,0:T(8,128)} %copy-done.6), custom_call_target="tpu_custom_call" | custom-call | bytes 6291456 | tf_op jit(solution)/shard_map/columns/pallas_call | solution.py:332
  128.7 2.4 collective-permute-done.17
  132.1 2.8 %copy-done.2 = f32[32,3,128,128]{3,2,1,0:T(8,128)S(1)} copy-done((f32[32,3,128,128]{3,2,1,0:T(8,128)S(1)}, f32[32,3,128,128]{3,2,1,0:T(8,128)}, u32[]{:S(2)}) %copy-start.2) | copy-done | bytes 6291480
  134.9 20.1 %density.3 = f32[32,128]{1,0:T(8,128)} custom-call(s32[144]{0:T(256)S(1)} %convert_reduce_fusion.counts_ref, f32[144,8,128]{2,1,0:T(8,128)S(1)} %bitcast.29, f32[32,3,128,128]{3,2,1,0:T(8,128)S(1)} %copy-done.2), custom_call_target="tpu_custom_call" | custom-call | tf_op jit(solution)/shard_map/density/pallas_call | solution.py:345
  160.5 5.9 %collective-permute-start.21 = (f32[4,1,4,128]{3,2,1,0:T(4,128)S(1)}, f32[4,1,4,128]{3,2,1,0:T(4,128)S(1)}, u32[]{:S(2)}, u32[]{:S(2)}) collective-permute-start(f32[4,1,4,128]{3,2,1,0:T(4,128)S(1)} %get-tuple-element.33), channel_id=1, source_target_pairs={{4,0},{8,4},{12,8},{16,12},{20,16},{24,20},{28,24},{0,28},{5,1},{9... | collective-permute-start | bytes 24584 | tf_op jit(solution)/shard_map/ppermute | solution.py:388
  168.9 2.0 collective-permute-start.23
  171.0 4.8 %columns.7.speed_ref = f32[32,3,128,128]{3,2,1,0:T(8,128)} custom-call(f32[32,8,128]{2,1,0:T(8,128)} %copy-done.6), custom_call_target="tpu_custom_call" | custom-call | bytes 6291456 | tf_op jit(solution)/shard_map/columns/pallas_call | solution.py:332
  176.4 2.8 %copy-done.3 = f32[32,3,128,128]{3,2,1,0:T(8,128)S(1)} copy-done((f32[32,3,128,128]{3,2,1,0:T(8,128)S(1)}, f32[32,3,128,128]{3,2,1,0:T(8,128)}, u32[]{:S(2)}) %copy-start.3) | copy-done | bytes 6291480
  179.2 2.8 %copy-done.5 = f32[32,3,128,128]{3,2,1,0:T(8,128)S(1)} copy-done((f32[32,3,128,128]{3,2,1,0:T(8,128)S(1)}, f32[32,3,128,128]{3,2,1,0:T(8,128)}, u32[]{:S(2)}) %copy-start.5) | copy-done | bytes 6291480
  182.0 34.2 %accel.3 = f32[128,8,128]{2,1,0:T(8,128)S(1)} custom-call(s32[144]{0:T(256)S(1)} %convert_reduce_fusion.counts_ref, s32[32]{0:T(128)S(1)} %multiply_add_fusion.where_ref, f32[144,8,128]{2,1,0:T(8,128)S(1)} %bitcast.30, f32[144,128]{1,0:T(8,128)S(1)} %reshape.110.rho_ref, f32[32,3,128,128]{3,2,1,0:T(8,128)S(1)} %copy-done.3, f32[32,3,128,128]{3,2,1,0:T(8,128)S(1)} %copy-done.5), custom_call_target="tpu_custom_call" | custom-call | tf_op jit(solution)/shard_map/accel/pallas_call | solution.py:362
  216.2 43.2 %all_to_all.5 = f32[128,8,128]{2,1,0:T(8,128)S(1)} all-to-all(f32[128,8,128]{2,1,0:T(8,128)S(1)} %accel.3), channel_id=1, replica_groups=mesh['gx'=8,'gy'=8,'gz'=4] {'gx','gy'}, dimensions={0} | all-to-all | bytes 1048576 | tf_op jit(solution)/shard_map/all_to_all | solution.py:445
  (79 shorter events, 26.7 us)
Async XLA Ops:
  3.2 3.7 %collective-permute-start = (f32[1,4,4,8,128]{4,2,1,0,3:T(4,128)S(1)}, f32[1,4,4,8,128]{4,2,1,0,3:T(4,128)S(1)}, u32[]{:S(2)}, u32[]{:S(2)}) collective-permute-start(f32[1,4,4,8,128]{4,2,1,0,3:T(4,128)S(1)} %get-tuple-element.26), channel_id=1, source_target_pairs={{0,32},{32,64},{64,96},{96,128},{128,160},{160,192},{192,224},{224... | collective-permute-start | bytes 196616 | tf_op jit(solution)/shard_map/ppermute | solution.py:387
  3.2 3.7 %collective-permute-start.1 = (f32[1,4,4,8,128]{4,2,1,0,3:T(4,128)S(1)}, f32[1,4,4,8,128]{4,2,1,0,3:T(4,128)S(1)}, u32[]{:S(2)}, u32[]{:S(2)}) collective-permute-start(f32[1,4,4,8,128]{4,2,1,0,3:T(4,128)S(1)} %get-tuple-element.27), channel_id=1, source_target_pairs={{32,0},{64,32},{96,64},{128,96},{160,128},{192,160},{224,192},{0,2... | collective-permute-start | bytes 196616 | tf_op jit(solution)/shard_map/ppermute | solution.py:388
  7.0 8.2 %collective-permute-start.2 = (f32[4,1,4,8,128]{4,2,1,0,3:T(4,128)S(1)}, f32[4,1,4,8,128]{4,2,1,0,3:T(4,128)S(1)}, u32[]{:S(2)}, u32[]{:S(2)}) collective-permute-start(f32[4,1,4,8,128]{4,2,1,0,3:T(4,128)S(1)} %get-tuple-element.22), channel_id=1, source_target_pairs={{0,4},{4,8},{8,12},{12,16},{16,20},{20,24},{24,28},{28,0},{1,5},{5... | collective-permute-start | bytes 196616 | tf_op jit(solution)/shard_map/ppermute | solution.py:387
  9.0 6.2 %collective-permute-start.3 = (f32[4,1,4,8,128]{4,2,1,0,3:T(4,128)S(1)}, f32[4,1,4,8,128]{4,2,1,0,3:T(4,128)S(1)}, u32[]{:S(2)}, u32[]{:S(2)}) collective-permute-start(f32[4,1,4,8,128]{4,2,1,0,3:T(4,128)S(1)} %get-tuple-element.23), channel_id=1, source_target_pairs={{4,0},{8,4},{12,8},{16,12},{20,16},{24,20},{28,24},{0,28},{5,1},{9... | collective-permute-start | bytes 196616 | tf_op jit(solution)/shard_map/ppermute | solution.py:388
  15.3 7.9 %collective-permute-start.4 = (f32[4,6,1,8,128]{4,2,1,0,3:T(1,128)S(1)}, f32[4,6,1,8,128]{4,2,1,0,3:T(1,128)S(1)}, u32[]{:S(2)}, u32[]{:S(2)}) collective-permute-start(f32[4,6,1,8,128]{4,2,1,0,3:T(1,128)S(1)} %get-tuple-element.18), channel_id=1, source_target_pairs={{0,1},{1,2},{2,3},{3,0},{4,5},{5,6},{6,7},{7,4},{8,9},{9,10},{10,1... | collective-permute-start | bytes 294920 | tf_op jit(solution)/shard_map/ppermute | solution.py:387
  16.9 6.3 %collective-permute-start.5 = (f32[4,6,1,8,128]{4,2,1,0,3:T(1,128)S(1)}, f32[4,6,1,8,128]{4,2,1,0,3:T(1,128)S(1)}, u32[]{:S(2)}, u32[]{:S(2)}) collective-permute-start(f32[4,6,1,8,128]{4,2,1,0,3:T(1,128)S(1)} %get-tuple-element.19), channel_id=1, source_target_pairs={{1,0},{2,1},{3,2},{0,3},{5,4},{6,5},{7,6},{4,7},{9,8},{10,9},{11,1... | collective-permute-start | bytes 294920 | tf_op jit(solution)/shard_map/ppermute | solution.py:388
  24.1 2.8 %copy-start = (f32[32,3,128,128]{3,2,1,0:T(8,128)S(1)}, f32[32,3,128,128]{3,2,1,0:T(8,128)}, u32[]{:S(2)}) copy-start(f32[32,3,128,128]{3,2,1,0:T(8,128)} %columns.4.wide_ref) | copy-start | bytes 18874372
  46.4 4.5 %collective-permute-start.7 = (f32[1,4,4,128]{3,2,1,0:T(4,128)S(1)}, f32[1,4,4,128]{3,2,1,0:T(4,128)S(1)}, u32[]{:S(2)}, u32[]{:S(2)}) collective-permute-start(f32[1,4,4,128]{3,2,1,0:T(4,128)S(1)} %bitcast.46), channel_id=1, source_target_pairs={{32,0},{64,32},{96,64},{128,96},{160,128},{192,160},{224,192},{0,2... | collective-permute-start | bytes 24584 | tf_op jit(solution)/shard_map/ppermute | solution.py:388
  49.5 3.1 %collective-permute-start.6 = (f32[1,4,4,128]{3,2,1,0:T(4,128)S(1)}, f32[1,4,4,128]{3,2,1,0:T(4,128)S(1)}, u32[]{:S(2)}, u32[]{:S(2)}) collective-permute-start(f32[1,4,4,128]{3,2,1,0:T(4,128)S(1)} %bitcast.44), channel_id=1, source_target_pairs={{0,32},{32,64},{64,96},{96,128},{128,160},{160,192},{192,224},{224... | collective-permute-start | bytes 24584 | tf_op jit(solution)/shard_map/ppermute | solution.py:387
  52.6 4.9 %collective-permute-start.8 = (f32[4,1,4,128]{3,2,1,0:T(4,128)S(1)}, f32[4,1,4,128]{3,2,1,0:T(4,128)S(1)}, u32[]{:S(2)}, u32[]{:S(2)}) collective-permute-start(f32[4,1,4,128]{3,2,1,0:T(4,128)S(1)} %get-tuple-element.34), channel_id=1, source_target_pairs={{0,4},{4,8},{8,12},{12,16},{16,20},{20,24},{24,28},{28,0},{1,5},{5... | collective-permute-start | bytes 24584 | tf_op jit(solution)/shard_map/ppermute | solution.py:387
  52.6 4.9 %collective-permute-start.9 = (f32[4,1,4,128]{3,2,1,0:T(4,128)S(1)}, f32[4,1,4,128]{3,2,1,0:T(4,128)S(1)}, u32[]{:S(2)}, u32[]{:S(2)}) collective-permute-start(f32[4,1,4,128]{3,2,1,0:T(4,128)S(1)} %get-tuple-element.35), channel_id=1, source_target_pairs={{4,0},{8,4},{12,8},{16,12},{20,16},{24,20},{28,24},{0,28},{5,1},{9... | collective-permute-start | bytes 24584 | tf_op jit(solution)/shard_map/ppermute | solution.py:388
  57.5 7.5 %collective-permute-start.10 = (f32[4,6,1,128]{3,2,1,0:T(1,128)S(1)}, f32[4,6,1,128]{3,2,1,0:T(1,128)S(1)}, u32[]{:S(2)}, u32[]{:S(2)}) collective-permute-start(f32[4,6,1,128]{3,2,1,0:T(1,128)S(1)} %get-tuple-element.30), channel_id=1, source_target_pairs={{0,1},{1,2},{2,3},{3,0},{4,5},{5,6},{6,7},{7,4},{8,9},{9,10},{10,1... | collective-permute-start | bytes 36872 | tf_op jit(solution)/shard_map/ppermute | solution.py:387
  59.3 5.8 %collective-permute-start.11 = (f32[4,6,1,128]{3,2,1,0:T(1,128)S(1)}, f32[4,6,1,128]{3,2,1,0:T(1,128)S(1)}, u32[]{:S(2)}, u32[]{:S(2)}) collective-permute-start(f32[4,6,1,128]{3,2,1,0:T(1,128)S(1)} %get-tuple-element.31), channel_id=1, source_target_pairs={{1,0},{2,1},{3,2},{0,3},{5,4},{6,5},{7,6},{4,7},{9,8},{10,9},{11,1... | collective-permute-start | bytes 36872 | tf_op jit(solution)/shard_map/ppermute | solution.py:388
  65.1 2.8 %copy-start.1 = (f32[32,3,128,128]{3,2,1,0:T(8,128)S(1)}, f32[32,3,128,128]{3,2,1,0:T(8,128)}, u32[]{:S(2)}) copy-start(f32[32,3,128,128]{3,2,1,0:T(8,128)} %columns.4.wide_ref) | copy-start | bytes 18874372
  104.9 19.0 %copy-start.6 = (f32[32,8,128]{2,1,0:T(8,128)}, f32[32,8,128]{2,1,0:T(8,128)S(1)}, u32[]{:S(2)}) copy-start(f32[32,8,128]{2,1,0:T(8,128)S(1)} %accel.2.states_ref) | copy-start | bytes 393220
  104.9 5.2 %collective-permute-start.13 = (f32[1,4,4,8,128]{4,3,2,1,0:T(8,128)S(1)}, f32[1,4,4,8,128]{4,3,2,1,0:T(8,128)S(1)}, u32[]{:S(2)}, u32[]{:S(2)}) collective-permute-start(f32[1,4,4,8,128]{4,3,2,1,0:T(8,128)S(1)} %bitcast.42), channel_id=1, source_target_pairs={{32,0},{64,32},{96,64},{128,96},{160,128},{192,160},{224,192},{0,2... | collective-permute-start | bytes 196616 | tf_op jit(solution)/shard_map/ppermute | solution.py:388
  108.3 3.7 %collective-permute-start.12 = (f32[1,4,4,8,128]{4,3,2,1,0:T(8,128)S(1)}, f32[1,4,4,8,128]{4,3,2,1,0:T(8,128)S(1)}, u32[]{:S(2)}, u32[]{:S(2)}) collective-permute-start(f32[1,4,4,8,128]{4,3,2,1,0:T(8,128)S(1)} %bitcast.41), channel_id=1, source_target_pairs={{0,32},{32,64},{64,96},{96,128},{128,160},{160,192},{192,224},{224... | collective-permute-start | bytes 196616 | tf_op jit(solution)/shard_map/ppermute | solution.py:387
  112.0 6.8 %collective-permute-start.14 = (f32[4,1,4,8,128]{4,3,2,1,0:T(8,128)S(1)}, f32[4,1,4,8,128]{4,3,2,1,0:T(8,128)S(1)}, u32[]{:S(2)}, u32[]{:S(2)}) collective-permute-start(f32[4,1,4,8,128]{4,3,2,1,0:T(8,128)S(1)} %get-tuple-element.20), channel_id=1, source_target_pairs={{0,4},{4,8},{8,12},{12,16},{16,20},{20,24},{24,28},{28,0},{1,5},{5... | collective-permute-start | bytes 196616 | tf_op jit(solution)/shard_map/ppermute | solution.py:387
  114.8 4.3 %collective-permute-start.15 = (f32[4,1,4,8,128]{4,3,2,1,0:T(8,128)S(1)}, f32[4,1,4,8,128]{4,3,2,1,0:T(8,128)S(1)}, u32[]{:S(2)}, u32[]{:S(2)}) collective-permute-start(f32[4,1,4,8,128]{4,3,2,1,0:T(8,128)S(1)} %get-tuple-element.21), channel_id=1, source_target_pairs={{4,0},{8,4},{12,8},{16,12},{20,16},{24,20},{28,24},{0,28},{5,1},{9... | collective-permute-start | bytes 196616 | tf_op jit(solution)/shard_map/ppermute | solution.py:388
  119.1 9.6 %collective-permute-start.16 = (f32[4,6,1,8,128]{4,3,2,1,0:T(8,128)S(1)}, f32[4,6,1,8,128]{4,3,2,1,0:T(8,128)S(1)}, u32[]{:S(2)}, u32[]{:S(2)}) collective-permute-start(f32[4,6,1,8,128]{4,3,2,1,0:T(8,128)S(1)} %get-tuple-element.16), channel_id=1, source_target_pairs={{0,1},{1,2},{2,3},{3,0},{4,5},{5,6},{6,7},{7,4},{8,9},{9,10},{10,1... | collective-permute-start | bytes 294920 | tf_op jit(solution)/shard_map/ppermute | solution.py:387
  122.0 44.5 %copy-start.8 = (pred[32,32]{1,0:T(32,128)(4,1)S(1)}, pred[32,32]{1,0:T(32,128)(4,1)}, u32[]{:S(2)}) copy-start(pred[32,32]{1,0:T(32,128)(4,1)} %constant.33.clone) | copy-start | bytes 3076
  122.0 44.5 %copy-start.9 = (s32[32,1]{0,1:T(1,128)S(1)}, s32[32,1]{0,1:T(1,128)}, u32[]{:S(2)}) copy-start(s32[32,1]{0,1:T(1,128)} %param.10) | copy-start | bytes 388
  122.0 9.2 %collective-permute-start.17 = (f32[4,6,1,8,128]{4,3,2,1,0:T(8,128)S(1)}, f32[4,6,1,8,128]{4,3,2,1,0:T(8,128)S(1)}, u32[]{:S(2)}, u32[]{:S(2)}) collective-permute-start(f32[4,6,1,8,128]{4,3,2,1,0:T(8,128)S(1)} %get-tuple-element.17), channel_id=1, source_target_pairs={{1,0},{2,1},{3,2},{0,3},{5,4},{6,5},{7,6},{4,7},{9,8},{10,9},{11,1... | collective-permute-start | bytes 294920 | tf_op jit(solution)/shard_map/ppermute | solution.py:388
  132.1 2.8 %copy-start.2 = (f32[32,3,128,128]{3,2,1,0:T(8,128)S(1)}, f32[32,3,128,128]{3,2,1,0:T(8,128)}, u32[]{:S(2)}) copy-start(f32[32,3,128,128]{3,2,1,0:T(8,128)} %columns.6.wide_ref) | copy-start | bytes 18874372
  155.0 21.4 %copy-start.7 = (f32[32,128]{1,0:T(8,128)S(1)}, f32[32,128]{1,0:T(8,128)}, u32[]{:S(2)}) copy-start(f32[32,128]{1,0:T(8,128)} %density.3) | copy-start | bytes 49156
  155.8 1.4 collective-permute-start.19
  155.8 3.1 %collective-permute-start.18 = (f32[1,4,4,128]{3,2,1,0:T(4,128)S(1)}, f32[1,4,4,128]{3,2,1,0:T(4,128)S(1)}, u32[]{:S(2)}, u32[]{:S(2)}) collective-permute-start(f32[1,4,4,128]{3,2,1,0:T(4,128)S(1)} %bitcast.45), channel_id=1, source_target_pairs={{0,32},{32,64},{64,96},{96,128},{128,160},{160,192},{192,224},{224... | collective-permute-start | bytes 24584 | tf_op jit(solution)/shard_map/ppermute | solution.py:387
  159.6 8.4 %collective-permute-start.20 = (f32[4,1,4,128]{3,2,1,0:T(4,128)S(1)}, f32[4,1,4,128]{3,2,1,0:T(4,128)S(1)}, u32[]{:S(2)}, u32[]{:S(2)}) collective-permute-start(f32[4,1,4,128]{3,2,1,0:T(4,128)S(1)} %get-tuple-element.32), channel_id=1, source_target_pairs={{0,4},{4,8},{8,12},{12,16},{16,20},{20,24},{24,28},{28,0},{1,5},{5... | collective-permute-start | bytes 24584 | tf_op jit(solution)/shard_map/ppermute | solution.py:387
  160.5 7.5 %collective-permute-start.21 = (f32[4,1,4,128]{3,2,1,0:T(4,128)S(1)}, f32[4,1,4,128]{3,2,1,0:T(4,128)S(1)}, u32[]{:S(2)}, u32[]{:S(2)}) collective-permute-start(f32[4,1,4,128]{3,2,1,0:T(4,128)S(1)} %get-tuple-element.33), channel_id=1, source_target_pairs={{4,0},{8,4},{12,8},{16,12},{20,16},{24,20},{28,24},{0,28},{5,1},{9... | collective-permute-start | bytes 24584 | tf_op jit(solution)/shard_map/ppermute | solution.py:388
  168.8 6.9 %collective-permute-start.22 = (f32[4,6,1,128]{3,2,1,0:T(1,128)S(1)}, f32[4,6,1,128]{3,2,1,0:T(1,128)S(1)}, u32[]{:S(2)}, u32[]{:S(2)}) collective-permute-start(f32[4,6,1,128]{3,2,1,0:T(1,128)S(1)} %get-tuple-element.28), channel_id=1, source_target_pairs={{0,1},{1,2},{2,3},{3,0},{4,5},{5,6},{6,7},{7,4},{8,9},{9,10},{10,1... | collective-permute-start | bytes 36872 | tf_op jit(solution)/shard_map/ppermute | solution.py:387
  168.9 7.4 %collective-permute-start.23 = (f32[4,6,1,128]{3,2,1,0:T(1,128)S(1)}, f32[4,6,1,128]{3,2,1,0:T(1,128)S(1)}, u32[]{:S(2)}, u32[]{:S(2)}) collective-permute-start(f32[4,6,1,128]{3,2,1,0:T(1,128)S(1)} %get-tuple-element.29), channel_id=1, source_target_pairs={{1,0},{2,1},{3,2},{0,3},{5,4},{6,5},{7,6},{4,7},{9,8},{10,9},{11,1... | collective-permute-start | bytes 36872 | tf_op jit(solution)/shard_map/ppermute | solution.py:388
  176.4 2.8 %copy-start.3 = (f32[32,3,128,128]{3,2,1,0:T(8,128)S(1)}, f32[32,3,128,128]{3,2,1,0:T(8,128)}, u32[]{:S(2)}) copy-start(f32[32,3,128,128]{3,2,1,0:T(8,128)} %columns.6.wide_ref) | copy-start | bytes 18874372
  (2 other events, 5.6 us)
